TPU v7x, 128 devices: a whole 4x4x4 slice. The times are simulated.
128 devices in a mesh: grid: 16 (over z, x_lo, core), mem: 8 (over y, x_hi).
Axes of the slice: x: 4 (x_hi: 2, x_lo: 2; x = x_hi * 2 + x_lo), y: 4, z: 4, core: 2. Of those that a mesh axis runs over, the one named last changes fastest.
Arguments:
- alpha: float32 [40, 2, 1536, 768], P('mem', None, 'grid'), may hold values from -6 to 6
- perturbations: bfloat16 [40, 2, 1536, 768], P('mem', None, 'grid'), may hold values from -4.5 to 4.5
- innovation: float32 [2, 1536, 768], P(None, 'grid'), may hold values from -6.5 to 4.5
- obs_weight: float32 [2, 1536, 768], P(None, 'grid'), may hold values from 0.2 to 2
- diffusivity: float32 [2, 2], replicated, may hold values from 0.05 to 0.3, as said below
Outputs:
- gradient: float32 [40, 2, 1536, 768], P('mem', None, 'grid')
Inputs may be any that keep to these rules, and one draw needn't show every extreme that they name: diffusivity[0, level] lies between 0.24 and 0.3, diffusivity[1, level] between 0.05 and 0.2.
All inputs are finite; a program needn't handle non-finite values.
Results may differ from a plain program's by a relative error of at most 0.0003.
Values sent between devices are 32-bit elements; how exact they have to be, the bound alone decides.
A program may use at most 64 MiB of HBM per device.

v0:
```python
import jax
import jax.numpy as jnp
from jax import lax
from jax.sharding import PartitionSpec as P

STEPS = 10


def extended(block, sides, width):
    for axis, dim in sides:
        count = lax.axis_size(axis)
        forward = [(i, i + 1) for i in range(count - 1)]
        backward = [(target, source) for source, target in forward]
        low = lax.ppermute(
            lax.slice_in_dim(block, block.shape[dim] - width, None, axis=dim), axis, forward
        )
        high = lax.ppermute(lax.slice_in_dim(block, 0, width, axis=dim), axis, backward)
        block = jnp.concatenate([low, block, high], axis=dim)
    return block


def stencil(field, padded, kx, ky):
    along_x = padded[:, :, 2:] + padded[:, :, :-2] - 2.0 * field
    side = jnp.pad(field, ((0, 0), (0, 0), (0, 0), (1, 1)))
    along_y = side[:, :, :, 2:] + side[:, :, :, :-2] - 2.0 * field
    return field + kx * along_x + ky * along_y


def diffuse(field, diffusivity):
    kx = diffusivity[0][None, :, None, None]
    ky = diffusivity[1][None, :, None, None]
    for step in range(STEPS):
        padded = extended(field, (("grid", 2),), 1)
        field = stencil(field, padded, kx, ky)
    return field


def local(alpha, perturbations, innovation, obs_weight, diffusivity):
    localized = diffuse(alpha, diffusivity)
    partial_sum = jnp.sum(perturbations.astype(jnp.float32) * localized, axis=0)
    increment = lax.psum(partial_sum, "mem")
    misfit = obs_weight * (increment - innovation)
    forcing = perturbations.astype(jnp.float32) * misfit[None]
    return alpha + diffuse(forcing, diffusivity)


def solution(mesh):
    in_specs = (
        P("mem", None, "grid", None),
        P("mem", None, "grid", None),
        P(None, "grid", None),
        P(None, "grid", None),
        P(),
    )
    out_specs = P("mem", None, "grid", None)
    return jax.shard_map(local, mesh=mesh, in_specs=in_specs, out_specs=out_specs, check_vma=False)
```

profile of v0, /device:TPU:80, one launch (start us, length us, event | category | flops | bytes accessed | tf_op | source)
XLA Modules:
  0.0 319.8 jit_solution(2594992919333120272)
XLA Ops:
  7.6 2.4 collective-permute-start
  10.0 1.9 collective-permute-start.1
  12.8 3.4 %collective-permute-done.1 = f32[5,2,1,768]{3,2,1,0:T(1,128)S(1)} collective-permute-done((f32[5,2,1,768]{3,2,1,0:T(1,128)S(1)}, f32[5,2,1,768]{3,2,1,0:T(1,128)S(1)}, u32[]{:S(2)}, u32[]{:S(2)}) %collective-permute-start.1) | collective-permute-done | bytes 30752 | tf_op jit(solution)/shard_map/ppermute | solution.py:14
  16.1 7.3 %fusion.3 = f32[5,2,96,768]{3,2,1,0:T(8,128)S(1)} fusion(f32[5,2,96,768]{3,2,1,0:T(8,128)} %param.5, f32[5,2,1,768]{3,2,1,0:T(1,128)S(1)} %collective-permute-done.1, f32[5,2,1,768]{3,2,1,0:T(1,128)S(1)} %collective-permute-done, f32[2]{0:T(128)S(1)} %get-tuple-element.46, f32[2]{0:T(128)S(1)} %get-tuple-element.45), kind=kLoop, calls=%fused_computation.45 | loop fusion | flops 8110080 | bytes 5959696 | tf_op jit(solution)/shard_map/add | solution.py:26
  25.4 2.4 collective-permute-start.3
  27.8 3.7 %collective-permute-done.3 = f32[5,2,1,768]{3,2,1,0:T(1,128)S(1)} collective-permute-done((f32[5,2,1,768]{3,2,1,0:T(1,128)S(1)}, f32[5,2,1,768]{3,2,1,0:T(1,128)S(1)}, u32[]{:S(2)}, u32[]{:S(2)}) %collective-permute-start.3) | collective-permute-done | bytes 30752 | tf_op jit(solution)/shard_map/ppermute | solution.py:14
  31.5 2.4 fusion.7
  34.0 1.9 collective-permute-start.4
  35.9 2.4 collective-permute-start.5
  38.3 3.7 %collective-permute-done.5 = f32[5,2,1,768]{3,2,1,0:T(1,128)S(1)} collective-permute-done((f32[5,2,1,768]{3,2,1,0:T(1,128)S(1)}, f32[5,2,1,768]{3,2,1,0:T(1,128)S(1)}, u32[]{:S(2)}, u32[]{:S(2)}) %collective-permute-start.5) | collective-permute-done | bytes 30752 | tf_op jit(solution)/shard_map/ppermute | solution.py:14
  42.0 2.4 fusion.11
  46.4 2.4 collective-permute-start.7
  48.8 3.7 %collective-permute-done.7 = f32[5,2,1,768]{3,2,1,0:T(1,128)S(1)} collective-permute-done((f32[5,2,1,768]{3,2,1,0:T(1,128)S(1)}, f32[5,2,1,768]{3,2,1,0:T(1,128)S(1)}, u32[]{:S(2)}, u32[]{:S(2)}) %collective-permute-start.7) | collective-permute-done | bytes 30752 | tf_op jit(solution)/shard_map/ppermute | solution.py:14
  52.5 2.4 fusion.15
  56.8 2.4 collective-permute-start.9
  59.3 3.7 %collective-permute-done.9 = f32[5,2,1,768]{3,2,1,0:T(1,128)S(1)} collective-permute-done((f32[5,2,1,768]{3,2,1,0:T(1,128)S(1)}, f32[5,2,1,768]{3,2,1,0:T(1,128)S(1)}, u32[]{:S(2)}, u32[]{:S(2)}) %collective-permute-start.9) | collective-permute-done | bytes 30752 | tf_op jit(solution)/shard_map/ppermute | solution.py:14
  62.9 2.4 fusion.19
  67.3 2.4 collective-permute-start.11
  69.7 3.7 %collective-permute-done.11 = f32[5,2,1,768]{3,2,1,0:T(1,128)S(1)} collective-permute-done((f32[5,2,1,768]{3,2,1,0:T(1,128)S(1)}, f32[5,2,1,768]{3,2,1,0:T(1,128)S(1)}, u32[]{:S(2)}, u32[]{:S(2)}) %collective-permute-start.11) | collective-permute-done | bytes 30752 | tf_op jit(solution)/shard_map/ppermute | solution.py:14
  73.4 2.4 fusion.23
  77.8 2.4 collective-permute-start.13
  80.2 3.7 %collective-permute-done.13 = f32[5,2,1,768]{3,2,1,0:T(1,128)S(1)} collective-permute-done((f32[5,2,1,768]{3,2,1,0:T(1,128)S(1)}, f32[5,2,1,768]{3,2,1,0:T(1,128)S(1)}, u32[]{:S(2)}, u32[]{:S(2)}) %collective-permute-start.13) | collective-permute-done | bytes 30752 | tf_op jit(solution)/shard_map/ppermute | solution.py:14
  83.9 2.4 fusion.27
  88.2 2.4 collective-permute-start.15
  90.7 3.7 %collective-permute-done.15 = f32[5,2,1,768]{3,2,1,0:T(1,128)S(1)} collective-permute-done((f32[5,2,1,768]{3,2,1,0:T(1,128)S(1)}, f32[5,2,1,768]{3,2,1,0:T(1,128)S(1)}, u32[]{:S(2)}, u32[]{:S(2)}) %collective-permute-start.15) | collective-permute-done | bytes 30752 | tf_op jit(solution)/shard_map/ppermute | solution.py:14
  94.3 2.4 fusion.31
  98.7 2.5 collective-permute-start.17
  101.3 3.7 %collective-permute-done.17 = f32[5,2,1,768]{3,2,1,0:T(1,128)S(1)} collective-permute-done((f32[5,2,1,768]{3,2,1,0:T(1,128)S(1)}, f32[5,2,1,768]{3,2,1,0:T(1,128)S(1)}, u32[]{:S(2)}, u32[]{:S(2)}) %collective-permute-start.17) | collective-permute-done | bytes 30752 | tf_op jit(solution)/shard_map/ppermute | solution.py:14
  105.0 2.4 fusion.35
  107.4 2.1 collective-permute-start.18
  109.5 2.6 collective-permute-start.19
  112.1 3.5 %collective-permute-done.19 = f32[5,2,1,768]{3,2,1,0:T(1,128)S(1)} collective-permute-done((f32[5,2,1,768]{3,2,1,0:T(1,128)S(1)}, f32[5,2,1,768]{3,2,1,0:T(1,128)S(1)}, u32[]{:S(2)}, u32[]{:S(2)}) %collective-permute-start.19) | collective-permute-done | bytes 30752 | tf_op jit(solution)/shard_map/ppermute | solution.py:14
  115.6 3.3 %fusion.81 = f32[2,96,768]{2,1,0:T(8,128)} fusion(f32[5,2,96,768]{3,2,1,0:T(8,128)S(1)} %fusion.35, bf16[5,2,96,768]{3,2,1,0:T(8,128)(2,1)S(1)} %copy-done.1, f32[5,2,1,768]{3,2,1,0:T(1,128)S(1)} %collective-permute-done.19, f32[5,2,1,768]{3,2,1,0:T(1,128)S(1)} %collective-permute-done.18, f32[2]{0:T(128)S(1)} %get-tuple-element.46, f32[2]{0:T(128)S(1)} %get-tuple-element.45), kind=kLoop, calls=%fused_computation.123 | loop fusion | flops 10174464 | bytes 5074960 | tf_op jit(solution)/shard_map/reduce_sum | solution.py:40
  118.9 85.9 %all-reduce.22.cloned.1.call-done = f32[2,96,768]{2,1,0:T(8,128)} async-done(((f32[2,96,768]{2,1,0:T(8,128)}), f32[2,96,768]{2,1,0:T(8,128)}) %all-reduce.22.cloned.1.call-update) | async-done | bytes 589840 | tf_op jit(solution)/shard_map/psum | solution.py:41
  208.3 2.4 collective-permute-start.21
  210.7 3.7 %collective-permute-done.21 = f32[5,2,1,768]{3,2,1,0:T(1,128)S(1)} collective-permute-done((f32[5,2,1,768]{3,2,1,0:T(1,128)S(1)}, f32[5,2,1,768]{3,2,1,0:T(1,128)S(1)}, u32[]{:S(2)}, u32[]{:S(2)}) %collective-permute-start.21) | collective-permute-done | bytes 30752 | tf_op jit(solution)/shard_map/ppermute | solution.py:14
  214.4 2.4 fusion.43
  218.7 2.4 collective-permute-start.23
  221.2 3.7 %collective-permute-done.23 = f32[5,2,1,768]{3,2,1,0:T(1,128)S(1)} collective-permute-done((f32[5,2,1,768]{3,2,1,0:T(1,128)S(1)}, f32[5,2,1,768]{3,2,1,0:T(1,128)S(1)}, u32[]{:S(2)}, u32[]{:S(2)}) %collective-permute-start.23) | collective-permute-done | bytes 30752 | tf_op jit(solution)/shard_map/ppermute | solution.py:14
  224.8 2.4 fusion.47
  229.2 2.4 collective-permute-start.25
  231.6 3.7 %collective-permute-done.25 = f32[5,2,1,768]{3,2,1,0:T(1,128)S(1)} collective-permute-done((f32[5,2,1,768]{3,2,1,0:T(1,128)S(1)}, f32[5,2,1,768]{3,2,1,0:T(1,128)S(1)}, u32[]{:S(2)}, u32[]{:S(2)}) %collective-permute-start.25) | collective-permute-done | bytes 30752 | tf_op jit(solution)/shard_map/ppermute | solution.py:14
  235.3 2.4 fusion.51
  239.7 2.4 collective-permute-start.27
  242.1 3.7 %collective-permute-done.27 = f32[5,2,1,768]{3,2,1,0:T(1,128)S(1)} collective-permute-done((f32[5,2,1,768]{3,2,1,0:T(1,128)S(1)}, f32[5,2,1,768]{3,2,1,0:T(1,128)S(1)}, u32[]{:S(2)}, u32[]{:S(2)}) %collective-permute-start.27) | collective-permute-done | bytes 30752 | tf_op jit(solution)/shard_map/ppermute | solution.py:14
  245.8 2.4 fusion.55
  250.1 2.4 collective-permute-start.29
  252.6 3.7 %collective-permute-done.29 = f32[5,2,1,768]{3,2,1,0:T(1,128)S(1)} collective-permute-done((f32[5,2,1,768]{3,2,1,0:T(1,128)S(1)}, f32[5,2,1,768]{3,2,1,0:T(1,128)S(1)}, u32[]{:S(2)}, u32[]{:S(2)}) %collective-permute-start.29) | collective-permute-done | bytes 30752 | tf_op jit(solution)/shard_map/ppermute | solution.py:14
  256.2 2.4 fusion.59
  260.6 2.4 collective-permute-start.31
  263.0 3.7 %collective-permute-done.31 = f32[5,2,1,768]{3,2,1,0:T(1,128)S(1)} collective-permute-done((f32[5,2,1,768]{3,2,1,0:T(1,128)S(1)}, f32[5,2,1,768]{3,2,1,0:T(1,128)S(1)}, u32[]{:S(2)}, u32[]{:S(2)}) %collective-permute-start.31) | collective-permute-done | bytes 30752 | tf_op jit(solution)/shard_map/ppermute | solution.py:14
  266.7 2.4 fusion.63
  271.1 2.4 collective-permute-start.33
  273.5 3.7 %collective-permute-done.33 = f32[5,2,1,768]{3,2,1,0:T(1,128)S(1)} collective-permute-done((f32[5,2,1,768]{3,2,1,0:T(1,128)S(1)}, f32[5,2,1,768]{3,2,1,0:T(1,128)S(1)}, u32[]{:S(2)}, u32[]{:S(2)}) %collective-permute-start.33) | collective-permute-done | bytes 30752 | tf_op jit(solution)/shard_map/ppermute | solution.py:14
  277.2 2.4 fusion.67
  281.5 2.4 collective-permute-start.35
  284.0 3.7 %collective-permute-done.35 = f32[5,2,1,768]{3,2,1,0:T(1,128)S(1)} collective-permute-done((f32[5,2,1,768]{3,2,1,0:T(1,128)S(1)}, f32[5,2,1,768]{3,2,1,0:T(1,128)S(1)}, u32[]{:S(2)}, u32[]{:S(2)}) %collective-permute-start.35) | collective-permute-done | bytes 30752 | tf_op jit(solution)/shard_map/ppermute | solution.py:14
  287.7 2.4 fusion.71
  292.0 2.9 collective-permute-start.37
  294.9 3.5 %collective-permute-done.37 = f32[5,2,1,768]{3,2,1,0:T(1,128)S(1)} collective-permute-done((f32[5,2,1,768]{3,2,1,0:T(1,128)S(1)}, f32[5,2,1,768]{3,2,1,0:T(1,128)S(1)}, u32[]{:S(2)}, u32[]{:S(2)}) %collective-permute-start.37) | collective-permute-done | bytes 30752 | tf_op jit(solution)/shard_map/ppermute | solution.py:14
  298.4 2.4 fusion.75
  302.8 2.4 collective-permute-start.39
  305.2 3.7 %collective-permute-done.39 = f32[5,2,1,768]{3,2,1,0:T(1,128)S(1)} collective-permute-done((f32[5,2,1,768]{3,2,1,0:T(1,128)S(1)}, f32[5,2,1,768]{3,2,1,0:T(1,128)S(1)}, u32[]{:S(2)}, u32[]{:S(2)}) %collective-permute-start.39) | collective-permute-done | bytes 30752 | tf_op jit(solution)/shard_map/ppermute | solution.py:14
  308.9 4.1 %fusion.80 = f32[5,2,96,768]{3,2,1,0:T(8,128)} fusion(f32[5,2,96,768]{3,2,1,0:T(8,128)S(1)} %copy-done, f32[5,2,96,768]{3,2,1,0:T(8,128)S(1)} %fusion.75, f32[5,2,1,768]{3,2,1,0:T(1,128)S(1)} %collective-permute-done.39, f32[5,2,1,768]{3,2,1,0:T(1,128)S(1)} %collective-permute-done.38, f32[2]{0:T(128)S(1)} %get-tuple-element.46, f32[2]{0:T(128)S(1)} %get-tuple-element.45), kind=kLoop, calls=%fused_computation.122 | loop fusion | flops 8847360 | bytes 8908816 | tf_op jit(solution)/shard_map/add | solution.py:44
  (70 shorter events, 36.9 us)
Async XLA Ops:
  6.5 198.3 %all-reduce.22.cloned.1.call-start = ((), (), s32[]{:S(2)}) async-start(), calls=%async_computation | async-start | bytes 1179648 | tf_op jit(solution)/shard_map/psum | solution.py:41
  7.6 5.1 %collective-permute-start = (f32[5,2,1,768]{3,2,1,0:T(1,128)S(1)}, f32[5,2,1,768]{3,2,1,0:T(1,128)S(1)}, u32[]{:S(2)}, u32[]{:S(2)}) collective-permute-start(f32[5,2,1,768]{3,2,1,0:T(1,128)S(1)} %get-tuple-element.43), channel_id=1, source_target_pairs={{8,0},{16,8},{24,16},{32,24},{40,32},{48,40},{56,48},{64,56},{72,6... | collective-permute-start | bytes 92168 | tf_op jit(solution)/shard_map/ppermute | solution.py:17
  10.0 6.1 %collective-permute-start.1 = (f32[5,2,1,768]{3,2,1,0:T(1,128)S(1)}, f32[5,2,1,768]{3,2,1,0:T(1,128)S(1)}, u32[]{:S(2)}, u32[]{:S(2)}) collective-permute-start(f32[5,2,1,768]{3,2,1,0:T(1,128)S(1)} %get-tuple-element.44), channel_id=1, source_target_pairs={{0,8},{8,16},{16,24},{24,32},{32,40},{40,48},{48,56},{56,64},{64,7... | collective-permute-start | bytes 92168 | tf_op jit(solution)/shard_map/ppermute | solution.py:14
  23.5 4.3 %collective-permute-start.2 = (f32[5,2,1,768]{3,2,1,0:T(1,128)S(1)}, f32[5,2,1,768]{3,2,1,0:T(1,128)S(1)}, u32[]{:S(2)}, u32[]{:S(2)}) collective-permute-start(f32[5,2,1,768]{3,2,1,0:T(1,128)S(1)} %get-tuple-element.41), channel_id=1, source_target_pairs={{8,0},{16,8},{24,16},{32,24},{40,32},{48,40},{56,48},{64,56},{72,6... | collective-permute-start | bytes 92168 | tf_op jit(solution)/shard_map/ppermute | solution.py:17
  25.4 6.1 %collective-permute-start.3 = (f32[5,2,1,768]{3,2,1,0:T(1,128)S(1)}, f32[5,2,1,768]{3,2,1,0:T(1,128)S(1)}, u32[]{:S(2)}, u32[]{:S(2)}) collective-permute-start(f32[5,2,1,768]{3,2,1,0:T(1,128)S(1)} %get-tuple-element.42), channel_id=1, source_target_pairs={{0,8},{8,16},{16,24},{24,32},{32,40},{40,48},{48,56},{56,64},{64,7... | collective-permute-start | bytes 92168 | tf_op jit(solution)/shard_map/ppermute | solution.py:14
  34.0 4.3 %collective-permute-start.4 = (f32[5,2,1,768]{3,2,1,0:T(1,128)S(1)}, f32[5,2,1,768]{3,2,1,0:T(1,128)S(1)}, u32[]{:S(2)}, u32[]{:S(2)}) collective-permute-start(f32[5,2,1,768]{3,2,1,0:T(1,128)S(1)} %get-tuple-element.39), channel_id=1, source_target_pairs={{8,0},{16,8},{24,16},{32,24},{40,32},{48,40},{56,48},{64,56},{72,6... | collective-permute-start | bytes 92168 | tf_op jit(solution)/shard_map/ppermute | solution.py:17
  35.9 6.1 %collective-permute-start.5 = (f32[5,2,1,768]{3,2,1,0:T(1,128)S(1)}, f32[5,2,1,768]{3,2,1,0:T(1,128)S(1)}, u32[]{:S(2)}, u32[]{:S(2)}) collective-permute-start(f32[5,2,1,768]{3,2,1,0:T(1,128)S(1)} %get-tuple-element.40), channel_id=1, source_target_pairs={{0,8},{8,16},{16,24},{24,32},{32,40},{40,48},{48,56},{56,64},{64,7... | collective-permute-start | bytes 92168 | tf_op jit(solution)/shard_map/ppermute | solution.py:14
  44.4 4.3 %collective-permute-start.6 = (f32[5,2,1,768]{3,2,1,0:T(1,128)S(1)}, f32[5,2,1,768]{3,2,1,0:T(1,128)S(1)}, u32[]{:S(2)}, u32[]{:S(2)}) collective-permute-start(f32[5,2,1,768]{3,2,1,0:T(1,128)S(1)} %get-tuple-element.37), channel_id=1, source_target_pairs={{8,0},{16,8},{24,16},{32,24},{40,32},{48,40},{56,48},{64,56},{72,6... | collective-permute-start | bytes 92168 | tf_op jit(solution)/shard_map/ppermute | solution.py:17
  46.4 6.1 %collective-permute-start.7 = (f32[5,2,1,768]{3,2,1,0:T(1,128)S(1)}, f32[5,2,1,768]{3,2,1,0:T(1,128)S(1)}, u32[]{:S(2)}, u32[]{:S(2)}) collective-permute-start(f32[5,2,1,768]{3,2,1,0:T(1,128)S(1)} %get-tuple-element.38), channel_id=1, source_target_pairs={{0,8},{8,16},{16,24},{24,32},{32,40},{40,48},{48,56},{56,64},{64,7... | collective-permute-start | bytes 92168 | tf_op jit(solution)/shard_map/ppermute | solution.py:14
  54.9 4.3 %collective-permute-start.8 = (f32[5,2,1,768]{3,2,1,0:T(1,128)S(1)}, f32[5,2,1,768]{3,2,1,0:T(1,128)S(1)}, u32[]{:S(2)}, u32[]{:S(2)}) collective-permute-start(f32[5,2,1,768]{3,2,1,0:T(1,128)S(1)} %get-tuple-element.35), channel_id=1, source_target_pairs={{8,0},{16,8},{24,16},{32,24},{40,32},{48,40},{56,48},{64,56},{72,6... | collective-permute-start | bytes 92168 | tf_op jit(solution)/shard_map/ppermute | solution.py:17
  56.8 6.1 %collective-permute-start.9 = (f32[5,2,1,768]{3,2,1,0:T(1,128)S(1)}, f32[5,2,1,768]{3,2,1,0:T(1,128)S(1)}, u32[]{:S(2)}, u32[]{:S(2)}) collective-permute-start(f32[5,2,1,768]{3,2,1,0:T(1,128)S(1)} %get-tuple-element.36), channel_id=1, source_target_pairs={{0,8},{8,16},{16,24},{24,32},{32,40},{40,48},{48,56},{56,64},{64,7... | collective-permute-start | bytes 92168 | tf_op jit(solution)/shard_map/ppermute | solution.py:14
  65.4 4.3 %collective-permute-start.10 = (f32[5,2,1,768]{3,2,1,0:T(1,128)S(1)}, f32[5,2,1,768]{3,2,1,0:T(1,128)S(1)}, u32[]{:S(2)}, u32[]{:S(2)}) collective-permute-start(f32[5,2,1,768]{3,2,1,0:T(1,128)S(1)} %get-tuple-element.33), channel_id=1, source_target_pairs={{8,0},{16,8},{24,16},{32,24},{40,32},{48,40},{56,48},{64,56},{72,6... | collective-permute-start | bytes 92168 | tf_op jit(solution)/shard_map/ppermute | solution.py:17
  67.3 6.1 %collective-permute-start.11 = (f32[5,2,1,768]{3,2,1,0:T(1,128)S(1)}, f32[5,2,1,768]{3,2,1,0:T(1,128)S(1)}, u32[]{:S(2)}, u32[]{:S(2)}) collective-permute-start(f32[5,2,1,768]{3,2,1,0:T(1,128)S(1)} %get-tuple-element.34), channel_id=1, source_target_pairs={{0,8},{8,16},{16,24},{24,32},{32,40},{40,48},{48,56},{56,64},{64,7... | collective-permute-start | bytes 92168 | tf_op jit(solution)/shard_map/ppermute | solution.py:14
  75.8 4.3 %collective-permute-start.12 = (f32[5,2,1,768]{3,2,1,0:T(1,128)S(1)}, f32[5,2,1,768]{3,2,1,0:T(1,128)S(1)}, u32[]{:S(2)}, u32[]{:S(2)}) collective-permute-start(f32[5,2,1,768]{3,2,1,0:T(1,128)S(1)} %get-tuple-element.31), channel_id=1, source_target_pairs={{8,0},{16,8},{24,16},{32,24},{40,32},{48,40},{56,48},{64,56},{72,6... | collective-permute-start | bytes 92168 | tf_op jit(solution)/shard_map/ppermute | solution.py:17
  77.8 6.1 %collective-permute-start.13 = (f32[5,2,1,768]{3,2,1,0:T(1,128)S(1)}, f32[5,2,1,768]{3,2,1,0:T(1,128)S(1)}, u32[]{:S(2)}, u32[]{:S(2)}) collective-permute-start(f32[5,2,1,768]{3,2,1,0:T(1,128)S(1)} %get-tuple-element.32), channel_id=1, source_target_pairs={{0,8},{8,16},{16,24},{24,32},{32,40},{40,48},{48,56},{56,64},{64,7... | collective-permute-start | bytes 92168 | tf_op jit(solution)/shard_map/ppermute | solution.py:14
  86.3 4.3 %collective-permute-start.14 = (f32[5,2,1,768]{3,2,1,0:T(1,128)S(1)}, f32[5,2,1,768]{3,2,1,0:T(1,128)S(1)}, u32[]{:S(2)}, u32[]{:S(2)}) collective-permute-start(f32[5,2,1,768]{3,2,1,0:T(1,128)S(1)} %get-tuple-element.29), channel_id=1, source_target_pairs={{8,0},{16,8},{24,16},{32,24},{40,32},{48,40},{56,48},{64,56},{72,6... | collective-permute-start | bytes 92168 | tf_op jit(solution)/shard_map/ppermute | solution.py:17
  88.2 6.1 %collective-permute-start.15 = (f32[5,2,1,768]{3,2,1,0:T(1,128)S(1)}, f32[5,2,1,768]{3,2,1,0:T(1,128)S(1)}, u32[]{:S(2)}, u32[]{:S(2)}) collective-permute-start(f32[5,2,1,768]{3,2,1,0:T(1,128)S(1)} %get-tuple-element.30), channel_id=1, source_target_pairs={{0,8},{8,16},{16,24},{24,32},{32,40},{40,48},{48,56},{56,64},{64,7... | collective-permute-start | bytes 92168 | tf_op jit(solution)/shard_map/ppermute | solution.py:14
  96.8 4.5 %collective-permute-start.16 = (f32[5,2,1,768]{3,2,1,0:T(1,128)S(1)}, f32[5,2,1,768]{3,2,1,0:T(1,128)S(1)}, u32[]{:S(2)}, u32[]{:S(2)}) collective-permute-start(f32[5,2,1,768]{3,2,1,0:T(1,128)S(1)} %get-tuple-element.27), channel_id=1, source_target_pairs={{8,0},{16,8},{24,16},{32,24},{40,32},{48,40},{56,48},{64,56},{72,6... | collective-permute-start | bytes 92168 | tf_op jit(solution)/shard_map/ppermute | solution.py:17
  98.7 16.9 %copy-start.1 = (bf16[5,2,96,768]{3,2,1,0:T(8,128)(2,1)S(1)}, bf16[5,2,96,768]{3,2,1,0:T(8,128)(2,1)}, u32[]{:S(2)}) copy-start(bf16[5,2,96,768]{3,2,1,0:T(8,128)(2,1)} %param.6) | copy-start | bytes 4423684
  98.7 6.2 %collective-permute-start.17 = (f32[5,2,1,768]{3,2,1,0:T(1,128)S(1)}, f32[5,2,1,768]{3,2,1,0:T(1,128)S(1)}, u32[]{:S(2)}, u32[]{:S(2)}) collective-permute-start(f32[5,2,1,768]{3,2,1,0:T(1,128)S(1)} %get-tuple-element.28), channel_id=1, source_target_pairs={{0,8},{8,16},{16,24},{24,32},{32,40},{40,48},{48,56},{56,64},{64,7... | collective-permute-start | bytes 92168 | tf_op jit(solution)/shard_map/ppermute | solution.py:14
  107.3 97.5 %copy-start.2 = (f32[2,96,768]{2,1,0:T(8,128)S(1)}, f32[2,96,768]{2,1,0:T(8,128)}, u32[]{:S(2)}) copy-start(f32[2,96,768]{2,1,0:T(8,128)} %param.8) | copy-start | bytes 1769476
  107.3 97.5 %copy-start.3 = (f32[2,96,768]{2,1,0:T(8,128)S(1)}, f32[2,96,768]{2,1,0:T(8,128)}, u32[]{:S(2)}) copy-start(f32[2,96,768]{2,1,0:T(8,128)} %param.7) | copy-start | bytes 1769476
  107.4 4.7 %collective-permute-start.18 = (f32[5,2,1,768]{3,2,1,0:T(1,128)S(1)}, f32[5,2,1,768]{3,2,1,0:T(1,128)S(1)}, u32[]{:S(2)}, u32[]{:S(2)}) collective-permute-start(f32[5,2,1,768]{3,2,1,0:T(1,128)S(1)} %get-tuple-element.25), channel_id=1, source_target_pairs={{8,0},{16,8},{24,16},{32,24},{40,32},{48,40},{56,48},{64,56},{72,6... | collective-permute-start | bytes 92168 | tf_op jit(solution)/shard_map/ppermute | solution.py:17
  109.5 6.1 %collective-permute-start.19 = (f32[5,2,1,768]{3,2,1,0:T(1,128)S(1)}, f32[5,2,1,768]{3,2,1,0:T(1,128)S(1)}, u32[]{:S(2)}, u32[]{:S(2)}) collective-permute-start(f32[5,2,1,768]{3,2,1,0:T(1,128)S(1)} %get-tuple-element.26), channel_id=1, source_target_pairs={{0,8},{8,16},{16,24},{24,32},{32,40},{40,48},{48,56},{56,64},{64,7... | collective-permute-start | bytes 92168 | tf_op jit(solution)/shard_map/ppermute | solution.py:14
  206.3 4.3 %collective-permute-start.20 = (f32[5,2,1,768]{3,2,1,0:T(1,128)S(1)}, f32[5,2,1,768]{3,2,1,0:T(1,128)S(1)}, u32[]{:S(2)}, u32[]{:S(2)}) collective-permute-start(f32[5,2,1,768]{3,2,1,0:T(1,128)S(1)} %get-tuple-element.23), channel_id=1, source_target_pairs={{8,0},{16,8},{24,16},{32,24},{40,32},{48,40},{56,48},{64,56},{72,6... | collective-permute-start | bytes 92168 | tf_op jit(solution)/shard_map/ppermute | solution.py:17
  208.3 6.1 %collective-permute-start.21 = (f32[5,2,1,768]{3,2,1,0:T(1,128)S(1)}, f32[5,2,1,768]{3,2,1,0:T(1,128)S(1)}, u32[]{:S(2)}, u32[]{:S(2)}) collective-permute-start(f32[5,2,1,768]{3,2,1,0:T(1,128)S(1)} %get-tuple-element.24), channel_id=1, source_target_pairs={{0,8},{8,16},{16,24},{24,32},{32,40},{40,48},{48,56},{56,64},{64,7... | collective-permute-start | bytes 92168 | tf_op jit(solution)/shard_map/ppermute | solution.py:14
  216.8 4.3 %collective-permute-start.22 = (f32[5,2,1,768]{3,2,1,0:T(1,128)S(1)}, f32[5,2,1,768]{3,2,1,0:T(1,128)S(1)}, u32[]{:S(2)}, u32[]{:S(2)}) collective-permute-start(f32[5,2,1,768]{3,2,1,0:T(1,128)S(1)} %get-tuple-element.21), channel_id=1, source_target_pairs={{8,0},{16,8},{24,16},{32,24},{40,32},{48,40},{56,48},{64,56},{72,6... | collective-permute-start | bytes 92168 | tf_op jit(solution)/shard_map/ppermute | solution.py:17
  218.7 6.1 %collective-permute-start.23 = (f32[5,2,1,768]{3,2,1,0:T(1,128)S(1)}, f32[5,2,1,768]{3,2,1,0:T(1,128)S(1)}, u32[]{:S(2)}, u32[]{:S(2)}) collective-permute-start(f32[5,2,1,768]{3,2,1,0:T(1,128)S(1)} %get-tuple-element.22), channel_id=1, source_target_pairs={{0,8},{8,16},{16,24},{24,32},{32,40},{40,48},{48,56},{56,64},{64,7... | collective-permute-start | bytes 92168 | tf_op jit(solution)/shard_map/ppermute | solution.py:14
  227.3 4.3 %collective-permute-start.24 = (f32[5,2,1,768]{3,2,1,0:T(1,128)S(1)}, f32[5,2,1,768]{3,2,1,0:T(1,128)S(1)}, u32[]{:S(2)}, u32[]{:S(2)}) collective-permute-start(f32[5,2,1,768]{3,2,1,0:T(1,128)S(1)} %get-tuple-element.19), channel_id=1, source_target_pairs={{8,0},{16,8},{24,16},{32,24},{40,32},{48,40},{56,48},{64,56},{72,6... | collective-permute-start | bytes 92168 | tf_op jit(solution)/shard_map/ppermute | solution.py:17
  229.2 6.1 %collective-permute-start.25 = (f32[5,2,1,768]{3,2,1,0:T(1,128)S(1)}, f32[5,2,1,768]{3,2,1,0:T(1,128)S(1)}, u32[]{:S(2)}, u32[]{:S(2)}) collective-permute-start(f32[5,2,1,768]{3,2,1,0:T(1,128)S(1)} %get-tuple-element.20), channel_id=1, source_target_pairs={{0,8},{8,16},{16,24},{24,32},{32,40},{40,48},{48,56},{56,64},{64,7... | collective-permute-start | bytes 92168 | tf_op jit(solution)/shard_map/ppermute | solution.py:14
  237.7 4.3 %collective-permute-start.26 = (f32[5,2,1,768]{3,2,1,0:T(1,128)S(1)}, f32[5,2,1,768]{3,2,1,0:T(1,128)S(1)}, u32[]{:S(2)}, u32[]{:S(2)}) collective-permute-start(f32[5,2,1,768]{3,2,1,0:T(1,128)S(1)} %get-tuple-element.17), channel_id=1, source_target_pairs={{8,0},{16,8},{24,16},{32,24},{40,32},{48,40},{56,48},{64,56},{72,6... | collective-permute-start | bytes 92168 | tf_op jit(solution)/shard_map/ppermute | solution.py:17
  239.7 6.1 %collective-permute-start.27 = (f32[5,2,1,768]{3,2,1,0:T(1,128)S(1)}, f32[5,2,1,768]{3,2,1,0:T(1,128)S(1)}, u32[]{:S(2)}, u32[]{:S(2)}) collective-permute-start(f32[5,2,1,768]{3,2,1,0:T(1,128)S(1)} %get-tuple-element.18), channel_id=1, source_target_pairs={{0,8},{8,16},{16,24},{24,32},{32,40},{40,48},{48,56},{56,64},{64,7... | collective-permute-start | bytes 92168 | tf_op jit(solution)/shard_map/ppermute | solution.py:14
  248.2 4.3 %collective-permute-start.28 = (f32[5,2,1,768]{3,2,1,0:T(1,128)S(1)}, f32[5,2,1,768]{3,2,1,0:T(1,128)S(1)}, u32[]{:S(2)}, u32[]{:S(2)}) collective-permute-start(f32[5,2,1,768]{3,2,1,0:T(1,128)S(1)} %get-tuple-element.15), channel_id=1, source_target_pairs={{8,0},{16,8},{24,16},{32,24},{40,32},{48,40},{56,48},{64,56},{72,6... | collective-permute-start | bytes 92168 | tf_op jit(solution)/shard_map/ppermute | solution.py:17
  250.1 6.1 %collective-permute-start.29 = (f32[5,2,1,768]{3,2,1,0:T(1,128)S(1)}, f32[5,2,1,768]{3,2,1,0:T(1,128)S(1)}, u32[]{:S(2)}, u32[]{:S(2)}) collective-permute-start(f32[5,2,1,768]{3,2,1,0:T(1,128)S(1)} %get-tuple-element.16), channel_id=1, source_target_pairs={{0,8},{8,16},{16,24},{24,32},{32,40},{40,48},{48,56},{56,64},{64,7... | collective-permute-start | bytes 92168 | tf_op jit(solution)/shard_map/ppermute | solution.py:14
  258.7 4.3 %collective-permute-start.30 = (f32[5,2,1,768]{3,2,1,0:T(1,128)S(1)}, f32[5,2,1,768]{3,2,1,0:T(1,128)S(1)}, u32[]{:S(2)}, u32[]{:S(2)}) collective-permute-start(f32[5,2,1,768]{3,2,1,0:T(1,128)S(1)} %get-tuple-element.13), channel_id=1, source_target_pairs={{8,0},{16,8},{24,16},{32,24},{40,32},{48,40},{56,48},{64,56},{72,6... | collective-permute-start | bytes 92168 | tf_op jit(solution)/shard_map/ppermute | solution.py:17
  260.6 6.1 %collective-permute-start.31 = (f32[5,2,1,768]{3,2,1,0:T(1,128)S(1)}, f32[5,2,1,768]{3,2,1,0:T(1,128)S(1)}, u32[]{:S(2)}, u32[]{:S(2)}) collective-permute-start(f32[5,2,1,768]{3,2,1,0:T(1,128)S(1)} %get-tuple-element.14), channel_id=1, source_target_pairs={{0,8},{8,16},{16,24},{24,32},{32,40},{40,48},{48,56},{56,64},{64,7... | collective-permute-start | bytes 92168 | tf_op jit(solution)/shard_map/ppermute | solution.py:14
  269.1 4.3 %collective-permute-start.32 = (f32[5,2,1,768]{3,2,1,0:T(1,128)S(1)}, f32[5,2,1,768]{3,2,1,0:T(1,128)S(1)}, u32[]{:S(2)}, u32[]{:S(2)}) collective-permute-start(f32[5,2,1,768]{3,2,1,0:T(1,128)S(1)} %get-tuple-element.11), channel_id=1, source_target_pairs={{8,0},{16,8},{24,16},{32,24},{40,32},{48,40},{56,48},{64,56},{72,6... | collective-permute-start | bytes 92168 | tf_op jit(solution)/shard_map/ppermute | solution.py:17
  271.1 6.1 %collective-permute-start.33 = (f32[5,2,1,768]{3,2,1,0:T(1,128)S(1)}, f32[5,2,1,768]{3,2,1,0:T(1,128)S(1)}, u32[]{:S(2)}, u32[]{:S(2)}) collective-permute-start(f32[5,2,1,768]{3,2,1,0:T(1,128)S(1)} %get-tuple-element.12), channel_id=1, source_target_pairs={{0,8},{8,16},{16,24},{24,32},{32,40},{40,48},{48,56},{56,64},{64,7... | collective-permute-start | bytes 92168 | tf_op jit(solution)/shard_map/ppermute | solution.py:14
  279.6 4.3 %collective-permute-start.34 = (f32[5,2,1,768]{3,2,1,0:T(1,128)S(1)}, f32[5,2,1,768]{3,2,1,0:T(1,128)S(1)}, u32[]{:S(2)}, u32[]{:S(2)}) collective-permute-start(f32[5,2,1,768]{3,2,1,0:T(1,128)S(1)} %get-tuple-element.9), channel_id=1, source_target_pairs={{8,0},{16,8},{24,16},{32,24},{40,32},{48,40},{56,48},{64,56},{72,6... | collective-permute-start | bytes 92168 | tf_op jit(solution)/shard_map/ppermute | solution.py:17
  281.5 6.1 %collective-permute-start.35 = (f32[5,2,1,768]{3,2,1,0:T(1,128)S(1)}, f32[5,2,1,768]{3,2,1,0:T(1,128)S(1)}, u32[]{:S(2)}, u32[]{:S(2)}) collective-permute-start(f32[5,2,1,768]{3,2,1,0:T(1,128)S(1)} %get-tuple-element.10), channel_id=1, source_target_pairs={{0,8},{8,16},{16,24},{24,32},{32,40},{40,48},{48,56},{56,64},{64,7... | collective-permute-start | bytes 92168 | tf_op jit(solution)/shard_map/ppermute | solution.py:14
  290.1 4.8 %collective-permute-start.36 = (f32[5,2,1,768]{3,2,1,0:T(1,128)S(1)}, f32[5,2,1,768]{3,2,1,0:T(1,128)S(1)}, u32[]{:S(2)}, u32[]{:S(2)}) collective-permute-start(f32[5,2,1,768]{3,2,1,0:T(1,128)S(1)} %get-tuple-element.7), channel_id=1, source_target_pairs={{8,0},{16,8},{24,16},{32,24},{40,32},{48,40},{56,48},{64,56},{72,6... | collective-permute-start | bytes 92168 | tf_op jit(solution)/shard_map/ppermute | solution.py:17
  292.0 16.9 %copy-start = (f32[5,2,96,768]{3,2,1,0:T(8,128)S(1)}, f32[5,2,96,768]{3,2,1,0:T(8,128)}, u32[]{:S(2)}) copy-start(f32[5,2,96,768]{3,2,1,0:T(8,128)} %param.5) | copy-start | bytes 8847364
  292.0 6.4 %collective-permute-start.37 = (f32[5,2,1,768]{3,2,1,0:T(1,128)S(1)}, f32[5,2,1,768]{3,2,1,0:T(1,128)S(1)}, u32[]{:S(2)}, u32[]{:S(2)}) collective-permute-start(f32[5,2,1,768]{3,2,1,0:T(1,128)S(1)} %get-tuple-element.8), channel_id=1, source_target_pairs={{0,8},{8,16},{16,24},{24,32},{32,40},{40,48},{48,56},{56,64},{64,7... | collective-permute-start | bytes 92168 | tf_op jit(solution)/shard_map/ppermute | solution.py:14
  300.9 4.3 %collective-permute-start.38 = (f32[5,2,1,768]{3,2,1,0:T(1,128)S(1)}, f32[5,2,1,768]{3,2,1,0:T(1,128)S(1)}, u32[]{:S(2)}, u32[]{:S(2)}) collective-permute-start(f32[5,2,1,768]{3,2,1,0:T(1,128)S(1)} %get-tuple-element.5), channel_id=1, source_target_pairs={{8,0},{16,8},{24,16},{32,24},{40,32},{48,40},{56,48},{64,56},{72,6... | collective-permute-start | bytes 92168 | tf_op jit(solution)/shard_map/ppermute | solution.py:17
  302.8 6.1 %collective-permute-start.39 = (f32[5,2,1,768]{3,2,1,0:T(1,128)S(1)}, f32[5,2,1,768]{3,2,1,0:T(1,128)S(1)}, u32[]{:S(2)}, u32[]{:S(2)}) collective-permute-start(f32[5,2,1,768]{3,2,1,0:T(1,128)S(1)} %get-tuple-element.6), channel_id=1, source_target_pairs={{0,8},{8,16},{16,24},{24,32},{32,40},{40,48},{48,56},{56,64},{64,7... | collective-permute-start | bytes 92168 | tf_op jit(solution)/shard_map/ppermute | solution.py:14
Sparse Core Ops, SparseCore 0:
  119.0 85.7 all-reduce.21
where the time goes:
time: 324 us; the launch traced here: 320 us
  waiting for transfers between devices  159 us (49%)
  starting transfers between devices  87.5 us (27%)
  other arithmetic  56.4 us (17%)
  between operations  14.2 us (4%)
    psum x1, waiting for transfers between devices, local(): increment = lax.psum(partial_sum, 'mem')  85.9 us
    ppermute x20, waiting for transfers between devices, extended(): lax.ppermute(lax.slice_in_dim(block, block.shape[dim] - width, None, axis...  73 us
    ppermute x20, starting transfers between devices, extended(): lax.ppermute(lax.slice_in_dim(block, block.shape[dim] - width, None, axis...  48.5 us
    add x18, other arithmetic, stencil(): return field + kx * along_x + ky * along_y  47.6 us
    ppermute x20, starting transfers between devices, extended(): lax.ppermute(lax.slice_in_dim(block, 0, width, axis=dim), axis, backward)  39 us
  transfers between devices with their start and end apart: 41, of which 21 were waited for; matrix products, arithmetic and copies ran while one was open for 0% of the time, Pallas kernels for 0%

commit v1 on v0

v1 whole, which is shorter than its diff:
```python
import functools

import jax
import jax.numpy as jnp
import ml_dtypes
import numpy as np
from jax import lax
from jax.experimental import pallas as pl
from jax.experimental.pallas import tpu as pltpu
from jax.sharding import PartitionSpec as P

STEPS = 10
BLOCK = 128
HALO = 16
RUN = 97
PAD = 16
MESH = pl.DeviceIdType.MESH
F32 = jnp.float32
BF16 = jnp.bfloat16


def transforms(rows):
    index = np.arange(1, BLOCK + 1, dtype=np.float64)
    sine = np.sqrt(2.0 / (BLOCK + 1)) * np.sin(np.pi * np.outer(index, index) / (BLOCK + 1))
    none = np.zeros((HALO, BLOCK))
    sets = []
    for offset in (0, HALO, 2 * HALO):
        inner = sine[offset : offset + rows]
        low = sine[offset - HALO : offset] if offset else none
        high = sine[offset + rows : offset + rows + HALO] if offset < 2 * HALO else none
        wide = np.concatenate([inner, low, high])
        made = []
        for matrix in (inner, wide):
            big = matrix.astype(ml_dtypes.bfloat16)
            small = (matrix - big.astype(np.float64)).astype(ml_dtypes.bfloat16)
            nil = np.zeros_like(big)
            into = np.block([[big, small], [big, nil]])
            back = np.block([[big, big], [small, nil]])
            made.append((into, back))
        sets.append((made[0][0], made[1][1], made[1][0], made[0][1]))
    return [np.stack(each) for each in zip(*sets)], np.cos(np.pi * index / (BLOCK + 1))


def split(value):
    big = value.astype(BF16)
    return big, (value - big.astype(F32)).astype(BF16)


def march(source, target, beta, first, last, columns):
    levels = [{} for _ in range(STEPS + 1)]
    low, high, skew = -STEPS, RUN + STEPS, 1
    for front in range(low, high + STEPS * skew):
        for step in range(STEPS + 1):
            at = front - step * skew
            if step == 0:
                if at >= high:
                    continue
                value = source[pl.ds(PAD + at, 8, stride=RUN), :]
            else:
                if at - 1 < low + step - 1 or at + 1 >= high - step + 1:
                    continue
                before = levels[step - 1]
                value = (before[at - 1] + before[at + 1]) + beta * before[at]
                del before[at - 1]
            if step < STEPS:
                if at == -1:
                    value = jnp.where(first, 0.0, value)
                if at == columns - 7 * RUN:
                    value = jnp.where(last, 0.0, value)
            levels[step][at] = value
            if step == STEPS:
                target[pl.ds(at, 8, stride=RUN), :] = value


def kernel(
    tiles, groups, members, rows, columns,
    dif_ref, alpha_hbm, pert_hbm, inn_hbm, ow_hbm, w1f_hbm, w2f_hbm, w1a_hbm, w2a_hbm, cos_ref,
    out_hbm,
    alpha_v, pert_v, out_v, inn_v, ow_v, w1f, w2f, w1a, w2a,
    edge, ph, lh, part, halo_part, got, halo_got, mis, mis_halo,
    fs, gb, hb, gs, beta_v, scale_v,
    in_sem, w_sem, out_sem, ph_s, ph_r, rs_s, rs_r, rh_s, rh_r, ag_s, ag_r, ah_s, ah_r,
):
    fields = 2 * members
    g = lax.axis_index("grid")
    m = lax.axis_index("mem")
    quarter, half = m // 2, lax.rem(m, 2)
    chunk_rows, chunk_cols = rows // 4, columns // 2
    variant = (g + tiles - 2) // (tiles - 1) + g // (tiles - 1)
    has_low, has_high = g > 0, g < tiles - 1

    loads = []
    for i in range(fields):
        level, member = i // members, i % members
        loads.append(pltpu.make_async_copy(pert_hbm.at[member, level], pert_v.at[i], in_sem.at[0, i]))
    for i in range(fields):
        level, member = i // members, i % members
        loads.append(pltpu.make_async_copy(alpha_hbm.at[member, level], alpha_v.at[i], in_sem.at[1, i]))
    weights = []
    for n, (src, dst) in enumerate(((w1f_hbm, w1f), (w2f_hbm, w2f), (w1a_hbm, w1a), (w2a_hbm, w2a))):
        weights.append(pltpu.make_async_copy(src.at[variant], dst, w_sem.at[n]))
    r0 = pl.multiple_of(quarter * chunk_rows, 8)
    c0 = pl.multiple_of(half * chunk_cols, 128)
    window = (slice(None), pl.ds(r0, chunk_rows), pl.ds(c0, chunk_cols))
    weights.append(pltpu.make_async_copy(inn_hbm.at[window], inn_v, w_sem.at[4]))
    weights.append(pltpu.make_async_copy(ow_hbm.at[window], ow_v, w_sem.at[5]))
    for copy in loads[:fields] + weights[:4] + loads[fields:] + weights[4:]:
        copy.start()

    barrier = pltpu.get_barrier_semaphore()
    for k in range(1, groups):
        pl.semaphore_signal(barrier, 1, device_id=(g, lax.rem(m + k, groups)), device_id_type=MESH)

    @pl.when(has_low)
    def _():
        for p in range(groups):
            pl.semaphore_signal(barrier, 1, device_id=(g - 1, p), device_id_type=MESH)

    @pl.when(has_high)
    def _():
        for p in range(groups):
            pl.semaphore_signal(barrier, 1, device_id=(g + 1, p), device_id_type=MESH)

    part[...] = jnp.zeros_like(part)
    halo_part[...] = jnp.zeros_like(halo_part)
    for level in range(2):
        kx = jnp.full((8, BLOCK), dif_ref[0, level], F32)
        ky = jnp.full((8, BLOCK), dif_ref[1, level], F32)
        beta_v[level] = (1.0 - 2.0 * ky - 2.0 * kx + 2.0 * kx * cos_ref[...]) / ky
        square = ky * ky
        fourth = square * square
        scale_v[level] = fourth * fourth * square
    gb[...] = jnp.zeros_like(gb)

    @pl.when(g == 0)
    def _():
        ph[0] = jnp.zeros_like(ph[0])
        mis_halo[:, 0] = jnp.zeros_like(mis_halo[:, 0])

    @pl.when(g == tiles - 1)
    def _():
        ph[1] = jnp.zeros_like(ph[1])
        mis_halo[:, 1] = jnp.zeros_like(mis_halo[:, 1])

    for i in range(fields):
        loads[i].wait()
        edge[1, i] = pert_v[i, 0:HALO, :].astype(F32)
        edge[0, i] = pert_v[i, rows - HALO : rows, :].astype(F32)

    neighbours = jnp.minimum(g, 1) + jnp.minimum(tiles - 1 - g, 1)
    pl.semaphore_wait(barrier, groups - 1 + groups * neighbours)

    def edge_copy(level, side):
        piece = pl.ds(level * members, members)
        return pltpu.make_async_remote_copy(
            src_ref=edge.at[side, piece], dst_ref=ph.at[side, piece],
            send_sem=ph_s.at[level, side], recv_sem=ph_r.at[level, side],
            device_id=(g + 1 - 2 * side, m), device_id_type=MESH,
        )

    for level in range(2):

        @pl.when(has_high)
        def _():
            edge_copy(level, 0).start()

        @pl.when(has_low)
        def _():
            edge_copy(level, 1).start()

    for copy in weights:
        copy.wait()

    def rs_copy(level, k):
        peer = lax.rem(m + k, groups)
        return pltpu.make_async_remote_copy(
            src_ref=part.at[level, peer], dst_ref=got.at[level, m],
            send_sem=rs_s.at[level, k], recv_sem=rs_r.at[level, m],
            device_id=(g, peer), device_id_type=MESH,
        )

    def rh_copy(level, side, h):
        return pltpu.make_async_remote_copy(
            src_ref=halo_part.at[level, side, h], dst_ref=halo_got.at[level, m],
            send_sem=rh_s.at[level, side, h], recv_sem=rh_r.at[level, m],
            device_id=(g - 1 + 2 * side, (groups - 2) * (1 - side) + h), device_id_type=MESH,
        )

    def ag_copy(level, k):
        return pltpu.make_async_remote_copy(
            src_ref=mis.at[level, m], dst_ref=mis.at[level, m],
            send_sem=ag_s.at[level, k], recv_sem=ag_r.at[level, m],
            device_id=(g, lax.rem(m + k, groups)), device_id_type=MESH,
        )

    def ah_copy(level, side, p):
        first = (chunk_rows - HALO) * (1 - side)
        return pltpu.make_async_remote_copy(
            src_ref=mis.at[level, m, pl.ds(first, HALO)], dst_ref=mis_halo.at[level, side, half],
            send_sem=ah_s.at[level, side, p], recv_sem=ah_r.at[level, side, half],
            device_id=(g + 1 - 2 * side, p), device_id_type=MESH,
        )

    def landed(ref, sem):
        pltpu.make_async_copy(ref, ref, sem).wait()

    def send_sums(level):
        @pl.when(has_low)
        def _():
            landed(ph.at[0, pl.ds(level * members, members)], ph_r.at[level, 0])

        @pl.when(has_high)
        def _():
            landed(ph.at[1, pl.ds(level * members, members)], ph_r.at[level, 1])

        for h in range(2):
            cut = slice(h * chunk_cols, (h + 1) * chunk_cols)
            for side in range(2):
                total = None
                for f in range(members):
                    i = level * members + f
                    term = lh[i, side, :, cut] * ph[side, i, :, cut]
                    total = term if total is None else total + term
                halo_part[level, side, h] = total
        for k in range(1, groups):
            rs_copy(level, k).start()

        @pl.when(has_low)
        def _():
            for h in range(2):
                rh_copy(level, 0, h).start()

        @pl.when(has_high)
        def _():
            for h in range(2):
                rh_copy(level, 1, h).start()

    at_low = (quarter == 0) & has_low
    at_high = (quarter == 3) & has_high

    def send_misfit(level):
        for k in range(1, groups):
            p = lax.rem(m + k, groups)
            landed(got.at[level, p], rs_r.at[level, p])
        total = part[level, m]
        for k in range(1, groups):
            total = total + got[level, lax.rem(m + k, groups)]
        got[level, m] = total

        @pl.when(at_low)
        def _():
            for p in range(groups):
                landed(halo_got.at[level, p], rh_r.at[level, p])
            got[level, m, 0:HALO] = got[level, m, 0:HALO] + sum(halo_got[level, p] for p in range(groups))

        @pl.when(at_high)
        def _():
            for p in range(groups):
                landed(halo_got.at[level, p], rh_r.at[level, p])
            last = slice(chunk_rows - HALO, chunk_rows)
            got[level, m, last] = got[level, m, last] + sum(halo_got[level, p] for p in range(groups))

        scale = scale_v[level, 0:1, 0:1]
        mis[level, m] = ow_v[level] * (got[level, m] * scale - inn_v[level]) * scale
        for k in range(1, groups):
            ag_copy(level, k).start()

        @pl.when(at_low)
        def _():
            for p in range(groups):
                ah_copy(level, 1, p).start()

        @pl.when(at_high)
        def _():
            for p in range(groups):
                ah_copy(level, 0, p).start()

    def take_misfit(level):
        for k in range(1, groups):
            p = lax.rem(m + k, groups)
            landed(mis.at[level, p], ag_r.at[level, p])

        @pl.when(has_low)
        def _():
            for h in range(2):
                landed(mis_halo.at[level, 0, h], ah_r.at[level, 0, h])

        @pl.when(has_high)
        def _():
            for h in range(2):
                landed(mis_halo.at[level, 1, h], ah_r.at[level, 1, h])

    sub = lax.broadcasted_iota(jnp.int32, (8, BLOCK), 0)
    first, last = sub == 0, sub == 7
    wide = 256

    def to_modes(count, weight):
        for c in range(0, columns, wide):
            made = lax.dot_general(
                fs[0:count, c : c + wide], weight[...], (((0,), (0,)), ((), ())), preferred_element_type=F32
            )
            gb[PAD + c : PAD + c + wide, :] = made[:, :BLOCK] + made[:, BLOCK:]

    def modes_out():
        for c in range(0, columns, 128):
            big, small = split(hb[c : c + 128, :])
            gs[c : c + 128, 0:BLOCK] = big
            gs[c : c + 128, BLOCK:] = small

    def from_modes(weight, c):
        return lax.dot_general(
            weight[...], gs[c : c + wide, :], (((1,), (1,)), ((), ())), preferred_element_type=F32
        )

    def forward(i, carry):
        level = i // members
        pltpu.make_async_copy(alpha_hbm.at[0, 0], alpha_v.at[i], in_sem.at[1, i]).wait()
        for c in range(0, columns, 128):
            big, small = split(alpha_v[i, :, c : c + 128])
            fs[0:rows, c : c + 128] = big
            fs[rows : 2 * rows, c : c + 128] = small
        to_modes(2 * rows, w1f)
        march(gb, hb, beta_v[level], first, last, columns)
        modes_out()
        for c in range(0, columns, wide):
            made = from_modes(w2f, c)
            made = made[:BLOCK] + made[BLOCK:]
            lh[i, 0, :, c : c + wide] = made[rows : rows + HALO]
            lh[i, 1, :, c : c + wide] = made[rows + HALO :]
            for d in range(c, c + wide, 128):
                h, e = d // chunk_cols, d % chunk_cols
                term = made[:rows, d - c : d - c + 128] * pert_v[i, :, d : d + 128].astype(F32)
                for q in range(4):
                    spot = (level, 2 * q + h, slice(None), slice(e, e + 128))
                    part[spot] = part[spot] + term[q * chunk_rows : (q + 1) * chunk_rows]

        @pl.when(i == members - 1)
        def _():
            send_sums(0)

        @pl.when(i == fields - 2)
        def _():
            send_misfit(0)

        return carry

    lax.fori_loop(0, fields, forward, 0)
    send_sums(1)

    def adjoint(i, carry):
        level = i // members

        @pl.when(i == 0)
        def _():
            take_misfit(0)

        @pl.when(i == members - 2)
        def _():
            send_misfit(1)

        @pl.when(i == members)
        def _():
            take_misfit(1)

        for c in range(0, columns, 128):
            h, e = c // chunk_cols, c % chunk_cols
            weightless = pert_v[i, :, c : c + 128].astype(F32)
            pieces = []
            for q in range(4):
                pieces.append(
                    weightless[q * chunk_rows : (q + 1) * chunk_rows] * mis[level, 2 * q + h, :, e : e + 128]
                )
            for side in range(2):
                pieces.append(ph[side, i, :, c : c + 128] * mis_halo[level, side, h, :, e : e + 128])
            big, small = split(jnp.concatenate(pieces, axis=0))
            fs[0:BLOCK, c : c + 128] = big
            fs[BLOCK : 2 * BLOCK, c : c + 128] = small
        to_modes(2 * BLOCK, w1a)
        march(gb, hb, beta_v[level], first, last, columns)
        modes_out()
        for c in range(0, columns, wide):
            made = from_modes(w2a, c)
            out_v[i, :, c : c + wide] = alpha_v[i, :, c : c + wide] + (made[:rows] + made[rows:])
        pltpu.make_async_copy(out_v.at[i], out_hbm.at[lax.rem(i, members), level], out_sem.at[i]).start()
        return carry

    lax.fori_loop(0, fields, adjoint, 0)

    for i in range(fields):
        pltpu.make_async_copy(out_v.at[i], out_hbm.at[i % members, i // members], out_sem.at[i]).wait()
    for level in range(2):
        for k in range(1, groups):
            rs_copy(level, k).wait_send()
            ag_copy(level, k).wait_send()

        @pl.when(has_low)
        def _():
            edge_copy(level, 1).wait_send()
            for h in range(2):
                rh_copy(level, 0, h).wait_send()

        @pl.when(has_high)
        def _():
            edge_copy(level, 0).wait_send()
            for h in range(2):
                rh_copy(level, 1, h).wait_send()

        @pl.when(at_low)
        def _():
            for p in range(groups):
                ah_copy(level, 1, p).wait_send()

        @pl.when(at_high)
        def _():
            for p in range(groups):
                ah_copy(level, 0, p).wait_send()


def local(tiles, groups, alpha, perturbations, innovation, obs_weight, diffusivity):
    members, levels, rows, columns = alpha.shape
    fields = members * levels
    (w1f, w2f, w1a, w2a), cosine = transforms(rows)
    cosine = np.broadcast_to(cosine.astype(np.float32), (8, BLOCK))
    any_space = pl.BlockSpec(memory_space=pl.ANY)
    dma = pltpu.SemaphoreType.DMA
    chunk = (rows // 4, columns // 2)
    halo = (HALO, columns // 2)
    return pl.pallas_call(
        functools.partial(kernel, tiles, groups, members, rows, columns),
        out_shape=jax.ShapeDtypeStruct(alpha.shape, F32),
        in_specs=[pl.BlockSpec(memory_space=pltpu.SMEM)] + [any_space] * 8 + [pl.BlockSpec(memory_space=pltpu.VMEM)],
        out_specs=any_space,
        scratch_shapes=[
            pltpu.VMEM((fields, rows, columns), F32),
            pltpu.VMEM((fields, rows, columns), BF16),
            pltpu.VMEM((fields, rows, columns), F32),
            pltpu.VMEM((levels,) + chunk, F32),
            pltpu.VMEM((levels,) + chunk, F32),
            pltpu.VMEM(w1f.shape[1:], BF16),
            pltpu.VMEM(w2f.shape[1:], BF16),
            pltpu.VMEM(w1a.shape[1:], BF16),
            pltpu.VMEM(w2a.shape[1:], BF16),
            pltpu.VMEM((2, fields, HALO, columns), F32),
            pltpu.VMEM((2, fields, HALO, columns), F32),
            pltpu.VMEM((fields, 2, HALO, columns), F32),
            pltpu.VMEM((levels, groups) + chunk, F32),
            pltpu.VMEM((levels, 2, 2) + halo, F32),
            pltpu.VMEM((levels, groups) + chunk, F32),
            pltpu.VMEM((levels, groups) + halo, F32),
            pltpu.VMEM((levels, groups) + chunk, F32),
            pltpu.VMEM((levels, 2, 2) + halo, F32),
            pltpu.VMEM((2 * BLOCK, columns), BF16),
            pltpu.VMEM((PAD + 8 * RUN + PAD, BLOCK), F32),
            pltpu.VMEM((8 * RUN, BLOCK), F32),
            pltpu.VMEM((8 * RUN, 2 * BLOCK), BF16),
            pltpu.VMEM((levels, 8, BLOCK), F32),
            pltpu.VMEM((levels, 8, BLOCK), F32),
            dma((2, fields)),
            dma((6,)),
            dma((fields,)),
            dma((levels, 2)),
            dma((levels, 2)),
            dma((levels, groups)),
            dma((levels, groups)),
            dma((levels, 2, 2)),
            dma((levels, groups)),
            dma((levels, groups)),
            dma((levels, groups)),
            dma((levels, 2, groups)),
            dma((levels, 2, 2)),
        ],
        compiler_params=pltpu.CompilerParams(
            collective_id=0, has_side_effects=True, vmem_limit_bytes=48 * 2**20
        ),
    )(diffusivity, alpha, perturbations, innovation, obs_weight, w1f, w2f, w1a, w2a, cosine)


def solution(mesh):
    in_specs = (
        P("mem", None, "grid", None),
        P("mem", None, "grid", None),
        P(None, "grid", None),
        P(None, "grid", None),
        P(),
    )
    out_specs = P("mem", None, "grid", None)
    body = functools.partial(local, mesh.shape["grid"], mesh.shape["mem"])
    return jax.shard_map(body, mesh=mesh, in_specs=in_specs, out_specs=out_specs, check_vma=False)
```

time: 324 us -> 69.1 us (0.21)
  the two profiles are of different devices: /device:TPU:80 before, /device:TPU:27 now
where the time goes in v1:
time: 69.1 us; the launch traced here: 68.7 us
  Pallas kernels  56.3 us (81%)
  local copies, waits for them, and re-layouts  12.4 us (18%)
    pallas_call x1, Pallas kernels, local(): pl.pallas_call(functools.partial(kernel, tiles, groups, members, rows, co...  56.3 us
    unnamed x17, local copies, waits for them, and re-layouts  11.7 us

profile of v1, /device:TPU:27, one launch (start us, length us, event | category | flops | bytes accessed | tf_op | source)
XLA Modules:
  0.0 68.7 jit_solution(6639934375226431908)
XLA Ops:
  0.0 0.7 jit_solution_.3.cos_ref
  0.7 0.0 copy-start
  0.7 1.4 %copy-done = bf16[5,2,96,768]{3,2,1,0:T(8,128)(2,1)S(1)} copy-done((bf16[5,2,96,768]{3,2,1,0:T(8,128)(2,1)S(1)}, bf16[5,2,96,768]{3,2,1,0:T(8,128)(2,1)}, u32[]{:S(2)}) %copy-start) | copy-done | bytes 1474584
  2.0 0.0 copy-start.1
  2.0 1.1 %copy-done.1 = f32[2,96,768]{2,1,0:T(8,128)S(1)} copy-done((f32[2,96,768]{2,1,0:T(8,128)S(1)}, f32[2,96,768]{2,1,0:T(8,128)}, u32[]{:S(2)}) %copy-start.1) | copy-done | bytes 589848
  3.1 0.0 copy-start.2
  3.1 1.1 %copy-done.2 = f32[2,96,768]{2,1,0:T(8,128)S(1)} copy-done((f32[2,96,768]{2,1,0:T(8,128)S(1)}, f32[2,96,768]{2,1,0:T(8,128)}, u32[]{:S(2)}) %copy-start.2) | copy-done | bytes 589848
  4.2 0.0 copy-start.3
  4.2 1.0 %copy-done.3 = bf16[3,256,256]{2,1,0:T(8,128)(2,1)S(1)} copy-done((bf16[3,256,256]{2,1,0:T(8,128)(2,1)S(1)}, bf16[3,256,256]{2,1,0:T(8,128)(2,1)}, u32[]{:S(2)}) %copy-start.3) | copy-done | bytes 393240
  5.2 0.0 copy-start.4
  5.2 1.0 %copy-done.4 = bf16[3,256,256]{2,1,0:T(8,128)(2,1)S(1)} copy-done((bf16[3,256,256]{2,1,0:T(8,128)(2,1)S(1)}, bf16[3,256,256]{2,1,0:T(8,128)(2,1)}, u32[]{:S(2)}) %copy-start.4) | copy-done | bytes 393240
  6.2 0.0 copy-start.5
  6.2 1.0 %copy-done.5 = bf16[3,192,256]{2,1,0:T(8,128)(2,1)S(1)} copy-done((bf16[3,192,256]{2,1,0:T(8,128)(2,1)S(1)}, bf16[3,192,256]{2,1,0:T(8,128)(2,1)}, u32[]{:S(2)}) %copy-start.5) | copy-done | bytes 294936
  7.1 0.0 copy-start.6
  7.1 1.0 %copy-done.6 = bf16[3,192,256]{2,1,0:T(8,128)(2,1)S(1)} copy-done((bf16[3,192,256]{2,1,0:T(8,128)(2,1)S(1)}, bf16[3,192,256]{2,1,0:T(8,128)(2,1)}, u32[]{:S(2)}) %copy-start.6) | copy-done | bytes 294936
  8.1 0.0 copy-start.7
  8.1 0.7 copy-done.7
  8.8 56.3 %shard_map.100 = f32[5,2,96,768]{3,2,1,0:T(8,128)} custom-call(f32[2,2]{1,0:T(2,128)S(1)} %copy-done.7, f32[5,2,96,768]{3,2,1,0:T(8,128)} %alpha_hbm.1, bf16[5,2,96,768]{3,2,1,0:T(8,128)(2,1)S(1)} %copy-done, f32[2,96,768]{2,1,0:T(8,128)S(1)} %copy-done.1, f32[2,96,768]{2,1,0:T(8,128)S(1)} %copy-done.2, bf16[3,192,256]{2,1,0:T(8,128)(2,1)S(1)} %copy-done.6, ...), custom_call_target="tpu_custom_call" | custom-call | tf_op jit(solution)/shard_map/pallas_call | solution.py:428
  65.0 3.6 %copy.12 = f32[5,2,96,768]{3,2,1,0:T(8,128)} copy(f32[5,2,96,768]{3,2,1,0:T(8,128)} %shard_map.100) | data formatting | bytes 5898240
Async XLA Ops:
  0.7 1.4 %copy-start = (bf16[5,2,96,768]{3,2,1,0:T(8,128)(2,1)S(1)}, bf16[5,2,96,768]{3,2,1,0:T(8,128)(2,1)}, u32[]{:S(2)}) copy-start(bf16[5,2,96,768]{3,2,1,0:T(8,128)(2,1)} %pert_hbm.1) | copy-start | bytes 4423684
  2.0 1.1 %copy-start.1 = (f32[2,96,768]{2,1,0:T(8,128)S(1)}, f32[2,96,768]{2,1,0:T(8,128)}, u32[]{:S(2)}) copy-start(f32[2,96,768]{2,1,0:T(8,128)} %inn_hbm.1) | copy-start | bytes 1769476
  3.1 1.1 %copy-start.2 = (f32[2,96,768]{2,1,0:T(8,128)S(1)}, f32[2,96,768]{2,1,0:T(8,128)}, u32[]{:S(2)}) copy-start(f32[2,96,768]{2,1,0:T(8,128)} %ow_hbm.1) | copy-start | bytes 1769476
  4.2 1.0 %copy-start.3 = (bf16[3,256,256]{2,1,0:T(8,128)(2,1)S(1)}, bf16[3,256,256]{2,1,0:T(8,128)(2,1)}, u32[]{:S(2)}) copy-start(bf16[3,256,256]{2,1,0:T(8,128)(2,1)} %constant.12.clone.w1a_hbm) | copy-start | bytes 1179652
  5.2 1.0 %copy-start.4 = (bf16[3,256,256]{2,1,0:T(8,128)(2,1)S(1)}, bf16[3,256,256]{2,1,0:T(8,128)(2,1)}, u32[]{:S(2)}) copy-start(bf16[3,256,256]{2,1,0:T(8,128)(2,1)} %constant.11.clone.w2f_hbm) | copy-start | bytes 1179652
  6.2 1.0 %copy-start.5 = (bf16[3,192,256]{2,1,0:T(8,128)(2,1)S(1)}, bf16[3,192,256]{2,1,0:T(8,128)(2,1)}, u32[]{:S(2)}) copy-start(bf16[3,192,256]{2,1,0:T(8,128)(2,1)} %constant.13.clone.w2a_hbm) | copy-start | bytes 884740
  7.1 1.0 %copy-start.6 = (bf16[3,192,256]{2,1,0:T(8,128)(2,1)S(1)}, bf16[3,192,256]{2,1,0:T(8,128)(2,1)}, u32[]{:S(2)}) copy-start(bf16[3,192,256]{2,1,0:T(8,128)(2,1)} %constant.10.clone.w1f_hbm) | copy-start | bytes 884740
  8.1 0.7 copy-start.7

commit v2 on v1

--- a/solution.py
+++ b/solution.py
@@ -74,10 +74,10 @@
 
 def kernel(
     tiles, groups, members, rows, columns,
-    dif_ref, alpha_hbm, pert_hbm, inn_hbm, ow_hbm, w1f_hbm, w2f_hbm, w1a_hbm, w2a_hbm, cos_ref,
+    dif_ref, alpha_hbm, pert_hbm, inn_hbm, ow_hbm, w1f_hbm, w2f_hbm, w1a_hbm, w2a_hbm, cos_hbm,
     out_hbm,
-    alpha_v, pert_v, out_v, inn_v, ow_v, w1f, w2f, w1a, w2a,
-    edge, ph, lh, part, halo_part, got, halo_got, mis, mis_halo,
+    alpha_v, pert_v, out_v, inn_v, ow_v, cos_ref, w1f, w2f, w1a, w2a,
+    edge, edge_got, ph, lh, part, halo_part, got, halo_got, mis, mis_halo,
     fs, gb, hb, gs, beta_v, scale_v,
     in_sem, w_sem, out_sem, ph_s, ph_r, rs_s, rs_r, rh_s, rh_r, ag_s, ag_r, ah_s, ah_r,
 ):
@@ -96,6 +96,7 @@
     for i in range(fields):
         level, member = i // members, i % members
         loads.append(pltpu.make_async_copy(alpha_hbm.at[member, level], alpha_v.at[i], in_sem.at[1, i]))
+    cosines = pltpu.make_async_copy(cos_hbm, cos_ref, w_sem.at[6])
     weights = []
     for n, (src, dst) in enumerate(((w1f_hbm, w1f), (w2f_hbm, w2f), (w1a_hbm, w1a), (w2a_hbm, w2a))):
         weights.append(pltpu.make_async_copy(src.at[variant], dst, w_sem.at[n]))
@@ -104,7 +105,7 @@
     window = (slice(None), pl.ds(r0, chunk_rows), pl.ds(c0, chunk_cols))
     weights.append(pltpu.make_async_copy(inn_hbm.at[window], inn_v, w_sem.at[4]))
     weights.append(pltpu.make_async_copy(ow_hbm.at[window], ow_v, w_sem.at[5]))
-    for copy in loads[:fields] + weights[:4] + loads[fields:] + weights[4:]:
+    for copy in loads[:fields] + [cosines] + loads[fields : fields + 1] + weights[:4] + loads[fields + 1 :] + weights[4:]:
         copy.start()
 
     barrier = pltpu.get_barrier_semaphore()
@@ -113,16 +114,14 @@
 
     @pl.when(has_low)
     def _():
-        for p in range(groups):
-            pl.semaphore_signal(barrier, 1, device_id=(g - 1, p), device_id_type=MESH)
+        pl.semaphore_signal(barrier, 1, device_id=(g - 1, m), device_id_type=MESH)
 
     @pl.when(has_high)
     def _():
-        for p in range(groups):
-            pl.semaphore_signal(barrier, 1, device_id=(g + 1, p), device_id_type=MESH)
+        pl.semaphore_signal(barrier, 1, device_id=(g + 1, m), device_id_type=MESH)
 
     part[...] = jnp.zeros_like(part)
-    halo_part[...] = jnp.zeros_like(halo_part)
+    cosines.wait()
     for level in range(2):
         kx = jnp.full((8, BLOCK), dif_ref[0, level], F32)
         ky = jnp.full((8, BLOCK), dif_ref[1, level], F32)
@@ -131,35 +130,30 @@
         fourth = square * square
         scale_v[level] = fourth * fourth * square
     gb[...] = jnp.zeros_like(gb)
+    ph[...] = jnp.zeros_like(ph)
 
     @pl.when(g == 0)
     def _():
-        ph[0] = jnp.zeros_like(ph[0])
         mis_halo[:, 0] = jnp.zeros_like(mis_halo[:, 0])
 
     @pl.when(g == tiles - 1)
     def _():
-        ph[1] = jnp.zeros_like(ph[1])
         mis_halo[:, 1] = jnp.zeros_like(mis_halo[:, 1])
 
     for i in range(fields):
         loads[i].wait()
-        edge[1, i] = pert_v[i, 0:HALO, :].astype(F32)
-        edge[0, i] = pert_v[i, rows - HALO : rows, :].astype(F32)
-
-    neighbours = jnp.minimum(g, 1) + jnp.minimum(tiles - 1 - g, 1)
-    pl.semaphore_wait(barrier, groups - 1 + groups * neighbours)
+        level, at = i // members, STEPS * (i % members)
+        edge[1, level, at : at + STEPS] = pert_v[i, 0:HALO, :].astype(F32)[:STEPS]
+        edge[0, level, at : at + STEPS] = pert_v[i, rows - HALO : rows, :].astype(F32)[HALO - STEPS :]
 
     def edge_copy(level, side):
-        piece = pl.ds(level * members, members)
         return pltpu.make_async_remote_copy(
-            src_ref=edge.at[side, piece], dst_ref=ph.at[side, piece],
+            src_ref=edge.at[side, level], dst_ref=edge_got.at[side, level],
             send_sem=ph_s.at[level, side], recv_sem=ph_r.at[level, side],
             device_id=(g + 1 - 2 * side, m), device_id_type=MESH,
         )
 
-    for level in range(2):
-
+    def send_edges(level):
         @pl.when(has_high)
         def _():
             edge_copy(level, 0).start()
@@ -167,6 +161,20 @@
         @pl.when(has_low)
         def _():
             edge_copy(level, 1).start()
+
+    def edges_sent(level):
+        @pl.when(has_high)
+        def _():
+            edge_copy(level, 0).wait_send()
+
+        @pl.when(has_low)
+        def _():
+            edge_copy(level, 1).wait_send()
+
+    def start_exchange():
+        neighbours = jnp.minimum(g, 1) + jnp.minimum(tiles - 1 - g, 1)
+        pl.semaphore_wait(barrier, groups - 1 + neighbours)
+        send_edges(0)
 
     for copy in weights:
         copy.wait()
@@ -205,35 +213,29 @@
         pltpu.make_async_copy(ref, ref, sem).wait()
 
     def send_sums(level):
-        @pl.when(has_low)
-        def _():
-            landed(ph.at[0, pl.ds(level * members, members)], ph_r.at[level, 0])
-
-        @pl.when(has_high)
-        def _():
-            landed(ph.at[1, pl.ds(level * members, members)], ph_r.at[level, 1])
-
-        for h in range(2):
-            cut = slice(h * chunk_cols, (h + 1) * chunk_cols)
-            for side in range(2):
-                total = None
-                for f in range(members):
-                    i = level * members + f
-                    term = lh[i, side, :, cut] * ph[side, i, :, cut]
-                    total = term if total is None else total + term
-                halo_part[level, side, h] = total
         for k in range(1, groups):
             rs_copy(level, k).start()
 
-        @pl.when(has_low)
-        def _():
-            for h in range(2):
-                rh_copy(level, 0, h).start()
-
-        @pl.when(has_high)
-        def _():
-            for h in range(2):
-                rh_copy(level, 1, h).start()
+    def send_halo_sums(level):
+        for side, there in ((0, has_low), (1, has_high)):
+
+            @pl.when(there)
+            def _():
+                landed(edge_got.at[side, level], ph_r.at[level, side])
+                for f in range(members):
+                    value = edge_got[side, level, f * STEPS : (f + 1) * STEPS]
+                    start = (HALO - STEPS) * (1 - side)
+                    ph[side, level * members + f, start : start + STEPS] = value
+                for h in range(2):
+                    cut = slice(h * chunk_cols, (h + 1) * chunk_cols)
+                    total = None
+                    for f in range(members):
+                        i = level * members + f
+                        term = lh[i, side, :, cut] * ph[side, i, :, cut]
+                        total = term if total is None else total + term
+                    halo_part[level, side, h] = total
+                for h in range(2):
+                    rh_copy(level, side, h).start()
 
     at_low = (quarter == 0) & has_low
     at_high = (quarter == 3) & has_high
@@ -334,18 +336,31 @@
                     spot = (level, 2 * q + h, slice(None), slice(e, e + 128))
                     part[spot] = part[spot] + term[q * chunk_rows : (q + 1) * chunk_rows]
 
+        @pl.when(i == 0)
+        def _():
+            start_exchange()
+
+        @pl.when(i == members - 2)
+        def _():
+            edges_sent(0)
+            send_edges(1)
+
         @pl.when(i == members - 1)
         def _():
             send_sums(0)
 
-        @pl.when(i == fields - 2)
-        def _():
-            send_misfit(0)
+        @pl.when(i == members + 1)
+        def _():
+            send_halo_sums(0)
 
         return carry
 
     lax.fori_loop(0, fields, forward, 0)
     send_sums(1)
+    send_halo_sums(1)
+    send_misfit(0)
+    send_misfit(1)
+    edges_sent(1)
 
     def adjoint(i, carry):
         level = i // members
@@ -353,10 +368,6 @@
         @pl.when(i == 0)
         def _():
             take_misfit(0)
-
-        @pl.when(i == members - 2)
-        def _():
-            send_misfit(1)
 
         @pl.when(i == members)
         def _():
@@ -395,13 +406,11 @@
 
         @pl.when(has_low)
         def _():
-            edge_copy(level, 1).wait_send()
             for h in range(2):
                 rh_copy(level, 0, h).wait_send()
 
         @pl.when(has_high)
         def _():
-            edge_copy(level, 0).wait_send()
             for h in range(2):
                 rh_copy(level, 1, h).wait_send()
 
@@ -421,14 +430,15 @@
     fields = members * levels
     (w1f, w2f, w1a, w2a), cosine = transforms(rows)
     cosine = np.broadcast_to(cosine.astype(np.float32), (8, BLOCK))
-    any_space = pl.BlockSpec(memory_space=pl.ANY)
+    any_space = pl.BlockSpec(memory_space=pltpu.HBM)
     dma = pltpu.SemaphoreType.DMA
     chunk = (rows // 4, columns // 2)
     halo = (HALO, columns // 2)
+    packed = -(-STEPS * members // 8) * 8
     return pl.pallas_call(
         functools.partial(kernel, tiles, groups, members, rows, columns),
         out_shape=jax.ShapeDtypeStruct(alpha.shape, F32),
-        in_specs=[pl.BlockSpec(memory_space=pltpu.SMEM)] + [any_space] * 8 + [pl.BlockSpec(memory_space=pltpu.VMEM)],
+        in_specs=[pl.BlockSpec(memory_space=pltpu.SMEM)] + [any_space] * 9,
         out_specs=any_space,
         scratch_shapes=[
             pltpu.VMEM((fields, rows, columns), F32),
@@ -436,11 +446,13 @@
             pltpu.VMEM((fields, rows, columns), F32),
             pltpu.VMEM((levels,) + chunk, F32),
             pltpu.VMEM((levels,) + chunk, F32),
+            pltpu.VMEM(cosine.shape, F32),
             pltpu.VMEM(w1f.shape[1:], BF16),
             pltpu.VMEM(w2f.shape[1:], BF16),
             pltpu.VMEM(w1a.shape[1:], BF16),
             pltpu.VMEM(w2a.shape[1:], BF16),
-            pltpu.VMEM((2, fields, HALO, columns), F32),
+            pltpu.VMEM((2, levels, packed, columns), F32),
+            pltpu.VMEM((2, levels, packed, columns), F32),
             pltpu.VMEM((2, fields, HALO, columns), F32),
             pltpu.VMEM((fields, 2, HALO, columns), F32),
             pltpu.VMEM((levels, groups) + chunk, F32),
@@ -456,7 +468,7 @@
             pltpu.VMEM((levels, 8, BLOCK), F32),
             pltpu.VMEM((levels, 8, BLOCK), F32),
             dma((2, fields)),
-            dma((6,)),
+            dma((7,)),
             dma((fields,)),
             dma((levels, 2)),
             dma((levels, 2)),
@@ -470,7 +482,7 @@
             dma((levels, 2, 2)),
         ],
         compiler_params=pltpu.CompilerParams(
-            collective_id=0, has_side_effects=True, vmem_limit_bytes=48 * 2**20
+            collective_id=0, has_side_effects=True, vmem_limit_bytes=60 * 2**20
         ),
     )(diffusivity, alpha, perturbations, innovation, obs_weight, w1f, w2f, w1a, w2a, cosine)
 

time: 69.1 us -> 51.8 us (0.75)
  the two profiles are of different devices: /device:TPU:27 before, /device:TPU:98 now
where the time goes in v2:
time: 51.8 us; the launch traced here: 51.6 us
  Pallas kernels  46.7 us (90%)
  local copies, waits for them, and re-layouts  4.87 us (9%)
    pallas_call x1, Pallas kernels, local(): pl.pallas_call(functools.partial(kernel, tiles, groups, members, rows, co...  46.7 us
    unnamed x1, local copies, waits for them, and re-layouts  3.62 us
    another operation x1, local copies, waits for them, and re-layouts  1.25 us

profile of v2, /device:TPU:98, one launch (start us, length us, event | category | flops | bytes accessed | tf_op | source)
XLA Modules:
  0.0 51.6 jit_solution(17370823152860794537)
XLA Ops:
  0.0 1.2 %jit_solution_.3.cos_hbm = f32[8,128]{1,0:T(8,128)} broadcast(f32[128]{0:T(128)} %constant.14.clone), dimensions={1} | broadcast | bytes 4608 | tf_op jit(solution)
  1.2 46.7 %shard_map.100 = f32[5,2,96,768]{3,2,1,0:T(8,128)} custom-call(f32[2,2]{1,0:T(2,128)} %dif_ref.1, f32[5,2,96,768]{3,2,1,0:T(8,128)} %alpha_hbm.1, bf16[5,2,96,768]{3,2,1,0:T(8,128)(2,1)} %pert_hbm.1, f32[2,96,768]{2,1,0:T(8,128)} %inn_hbm.1, f32[2,96,768]{2,1,0:T(8,128)} %ow_hbm.1, bf16[3,192,256]{2,1,0:T(8,128)(2,1)} %constant.10.clone.w1f_hbm, ...), custom_call_target="tpu_custom_call" | custom-call | tf_op jit(solution)/shard_map/pallas_call | solution.py:438
  48.0 3.6 %copy.12 = f32[5,2,96,768]{3,2,1,0:T(8,128)} copy(f32[5,2,96,768]{3,2,1,0:T(8,128)} %shard_map.100) | data formatting | bytes 5898240

commit v3 on v2

v3 whole, which is shorter than its diff:
```python
import functools

import jax
import jax.numpy as jnp
import ml_dtypes
import numpy as np
from jax import lax
from jax.experimental import pallas as pl
from jax.experimental.pallas import tpu as pltpu
from jax.sharding import PartitionSpec as P

STEPS = 10
UNROLL = 5
BLOCK = 128
HALO = 16
RUN = 97
PAD = 16
MESH = pl.DeviceIdType.MESH
F32 = jnp.float32
BF16 = jnp.bfloat16


def transforms(rows):
    index = np.arange(1, BLOCK + 1, dtype=np.float64)
    sine = np.sqrt(2.0 / (BLOCK + 1)) * np.sin(np.pi * np.outer(index, index) / (BLOCK + 1))
    none = np.zeros((HALO, BLOCK))
    sets = []
    for offset in (0, HALO, 2 * HALO):
        inner = sine[offset : offset + rows]
        low = sine[offset - HALO : offset] if offset else none
        high = sine[offset + rows : offset + rows + HALO] if offset < 2 * HALO else none
        wide = np.concatenate([inner, low, high])
        made = []
        for matrix in (inner, wide):
            big = matrix.astype(ml_dtypes.bfloat16)
            small = (matrix - big.astype(np.float64)).astype(ml_dtypes.bfloat16)
            nil = np.zeros_like(big)
            into = np.block([[big, small], [big, nil]])
            back = np.block([[big, big], [small, nil]])
            made.append((into, back))
        sets.append((made[0][0], made[1][1], made[1][0], made[0][1]))
    return [np.stack(each) for each in zip(*sets)]


def split(value):
    big = value.astype(BF16)
    return big, (value - big.astype(F32)).astype(BF16)


def march(source, target, beta, first, last, columns):
    levels = [{} for _ in range(STEPS + 1)]
    low, high, skew = -STEPS, RUN + STEPS, 1
    for front in range(low, high + STEPS * skew):
        for step in range(STEPS + 1):
            at = front - step * skew
            if step == 0:
                if at >= high:
                    continue
                value = source[pl.ds(PAD + at, 8, stride=RUN), :]
            else:
                if at - 1 < low + step - 1 or at + 1 >= high - step + 1:
                    continue
                before = levels[step - 1]
                value = (before[at - 1] + before[at + 1]) + beta * before[at]
                del before[at - 1]
            if step < STEPS:
                if at == -1:
                    value = jnp.where(first, 0.0, value)
                if at == columns - 7 * RUN:
                    value = jnp.where(last, 0.0, value)
            levels[step][at] = value
            if step == STEPS:
                target[pl.ds(at, 8, stride=RUN), :] = value


def kernel(
    tiles, groups, members, rows, columns,
    dif_ref, alpha_hbm, pert_hbm, inn_hbm, ow_hbm, w1f_hbm, w2f_hbm, w1a_hbm, w2a_hbm,
    out_hbm,
    alpha_v, pert_v, out_v, inn_v, ow_v, w1f, w2f, w1a, w2a,
    edge, edge_got, ph, lh, part, halo_part, got, halo_got, mine, other, mis, mis_halo,
    fs, gb, hb, gs, beta_v, scale_v,
    in_sem, w_sem, out_sem, ph_s, ph_r, rs_s, rs_r, rh_s, rh_r, x_s, x_r, ag_s, ag_r, ah_s, ah_r,
):
    fields = 2 * members
    g = lax.axis_index("grid")
    m = lax.axis_index("mem")
    quarters = groups // 2
    quarter, half = m // 2, lax.rem(m, 2)
    chunk_rows = rows // quarters
    variant = (g + tiles - 2) // (tiles - 1) + g // (tiles - 1)
    has_low, has_high = g > 0, g < tiles - 1

    loads = []
    for i in range(fields):
        level, member = i // members, i % members
        loads.append(pltpu.make_async_copy(pert_hbm.at[member, level], pert_v.at[i], in_sem.at[0, i]))
    for i in range(fields):
        level, member = i // members, i % members
        loads.append(pltpu.make_async_copy(alpha_hbm.at[member, level], alpha_v.at[i], in_sem.at[1, i]))
    weights = []
    for n, (src, dst) in enumerate(((w1f_hbm, w1f), (w2f_hbm, w2f), (w1a_hbm, w1a), (w2a_hbm, w2a))):
        weights.append(pltpu.make_async_copy(src.at[variant], dst, w_sem.at[n]))
    window = (slice(None), pl.ds(pl.multiple_of(quarter * chunk_rows, 8), chunk_rows))
    weights.append(pltpu.make_async_copy(inn_hbm.at[window], inn_v, w_sem.at[4]))
    weights.append(pltpu.make_async_copy(ow_hbm.at[window], ow_v, w_sem.at[5]))
    for copy in loads[:fields] + loads[fields : fields + 1] + weights[:4] + loads[fields + 1 :] + weights[4:]:
        copy.start()

    barrier = pltpu.get_barrier_semaphore()
    for k in range(1, quarters):
        pl.semaphore_signal(barrier, 1, device_id=(g, lax.rem(m + 2 * k, groups)), device_id_type=MESH)
    pl.semaphore_signal(barrier, 1, device_id=(g, m + 1 - 2 * half), device_id_type=MESH)

    @pl.when(has_low)
    def _():
        pl.semaphore_signal(barrier, 1, device_id=(g - 1, m), device_id_type=MESH)

    @pl.when(has_high)
    def _():
        pl.semaphore_signal(barrier, 1, device_id=(g + 1, m), device_id_type=MESH)

    part[...] = jnp.zeros_like(part)
    mode = lax.broadcasted_iota(jnp.int32, (8, BLOCK), 1) + 1
    cosine = jnp.cos(mode.astype(F32) * (np.pi / (BLOCK + 1)))
    for level in range(2):
        kx = jnp.full((8, BLOCK), dif_ref[0, level], F32)
        ky = jnp.full((8, BLOCK), dif_ref[1, level], F32)
        beta_v[level] = (1.0 - 2.0 * ky - 2.0 * kx + 2.0 * kx * cosine) / ky
        square = ky * ky
        fourth = square * square
        scale_v[level] = fourth * fourth * square
    gb[...] = jnp.zeros_like(gb)
    ph[...] = jnp.zeros_like(ph)

    @pl.when(g == 0)
    def _():
        mis_halo[:, 0] = jnp.zeros_like(mis_halo[:, 0])

    @pl.when(g == tiles - 1)
    def _():
        mis_halo[:, 1] = jnp.zeros_like(mis_halo[:, 1])

    for i in range(fields):
        loads[i].wait()
        level, at = i // members, STEPS * (i % members)
        edge[1, level, at : at + STEPS] = pert_v[i, 0:HALO, :].astype(F32)[:STEPS]
        edge[0, level, at : at + STEPS] = pert_v[i, rows - HALO : rows, :].astype(F32)[HALO - STEPS :]

    def edge_copy(level, side):
        return pltpu.make_async_remote_copy(
            src_ref=edge.at[side, level], dst_ref=edge_got.at[side, level],
            send_sem=ph_s.at[level, side], recv_sem=ph_r.at[level, side],
            device_id=(g + 1 - 2 * side, m), device_id_type=MESH,
        )

    def send_edges(level):
        @pl.when(has_high)
        def _():
            edge_copy(level, 0).start()

        @pl.when(has_low)
        def _():
            edge_copy(level, 1).start()

    def edges_sent(level):
        @pl.when(has_high)
        def _():
            edge_copy(level, 0).wait_send()

        @pl.when(has_low)
        def _():
            edge_copy(level, 1).wait_send()

    def start_exchange():
        neighbours = jnp.minimum(g, 1) + jnp.minimum(tiles - 1 - g, 1)
        pl.semaphore_wait(barrier, quarters + neighbours)
        send_edges(0)

    for copy in weights:
        copy.wait()

    def rs_copy(level, k):
        peer = lax.rem(quarter + k, quarters)
        return pltpu.make_async_remote_copy(
            src_ref=part.at[level, peer], dst_ref=got.at[level, quarter],
            send_sem=rs_s.at[level, k], recv_sem=rs_r.at[level, quarter],
            device_id=(g, 2 * peer + half), device_id_type=MESH,
        )

    def rh_copy(level, side):
        return pltpu.make_async_remote_copy(
            src_ref=halo_part.at[level, side], dst_ref=halo_got.at[level, quarter],
            send_sem=rh_s.at[level, side], recv_sem=rh_r.at[level, quarter],
            device_id=(g - 1 + 2 * side, 2 * (quarters - 1) * (1 - side) + half), device_id_type=MESH,
        )

    def pair_copy(level):
        return pltpu.make_async_remote_copy(
            src_ref=mine.at[level], dst_ref=other.at[level],
            send_sem=x_s.at[level], recv_sem=x_r.at[level],
            device_id=(g, m + 1 - 2 * half), device_id_type=MESH,
        )

    def ag_copy(level, k):
        peer = lax.rem(quarter + k, quarters)
        return pltpu.make_async_remote_copy(
            src_ref=mis.at[level, quarter], dst_ref=mis.at[level, quarter],
            send_sem=ag_s.at[level, k], recv_sem=ag_r.at[level, quarter],
            device_id=(g, 2 * peer + half), device_id_type=MESH,
        )

    def ah_copy(level, side):
        first = (chunk_rows - HALO) * (1 - side)
        return pltpu.make_async_remote_copy(
            src_ref=mis.at[level, (quarters - 1) * (1 - side), pl.ds(first, HALO)], dst_ref=mis_halo.at[level, side],
            send_sem=ah_s.at[level, side], recv_sem=ah_r.at[level, side],
            device_id=(g + 1 - 2 * side, m), device_id_type=MESH,
        )

    def landed(ref, sem):
        pltpu.make_async_copy(ref, ref, sem).wait()

    def send_sums(level):
        for k in range(1, quarters):
            rs_copy(level, k).start()

    def send_halo_sums(level):
        for side, there in ((0, has_low), (1, has_high)):

            @pl.when(there)
            def _():
                landed(edge_got.at[side, level], ph_r.at[level, side])
                for f in range(members):
                    value = edge_got[side, level, f * STEPS : (f + 1) * STEPS]
                    start = (HALO - STEPS) * (1 - side)
                    ph[side, level * members + f, start : start + STEPS] = value
                total = None
                for f in range(members):
                    i = level * members + f
                    term = lh[i, side] * ph[side, i]
                    total = term if total is None else total + term
                halo_part[level, side] = total
                rh_copy(level, side).start()

    at_low = (quarter == 0) & has_low
    at_high = (quarter == quarters - 1) & has_high

    def swap_sums(level):
        peers = [lax.rem(quarter + k, quarters) for k in range(1, quarters)]
        for p in peers:
            landed(got.at[level, p], rs_r.at[level, p])
        total = part[level, quarter]
        for p in peers:
            total = total + got[level, p]
        mine[level] = total
        for there, first in ((at_low, 0), (at_high, chunk_rows - HALO)):

            @pl.when(there)
            def _():
                for p in range(quarters):
                    landed(halo_got.at[level, p], rh_r.at[level, p])
                spot = slice(first, first + HALO)
                mine[level, spot] = mine[level, spot] + sum(halo_got[level, p] for p in range(quarters))

        pair_copy(level).start()

    def send_misfit(level):
        landed(other.at[level], x_r.at[level])
        scale = scale_v[level, 0:1, 0:1]
        mis[level, quarter] = ow_v[level] * ((mine[level] + other[level]) * scale - inn_v[level]) * scale
        for k in range(1, quarters):
            ag_copy(level, k).start()

    def take_misfit(level):
        for p in (0, quarters - 1):

            @pl.when(quarter != p)
            def _():
                landed(mis.at[level, p], ag_r.at[level, p])

            @pl.when(has_low if p == 0 else has_high)
            def _():
                ah_copy(level, 1 if p == 0 else 0).start()

        for p in range(1, quarters - 1):

            @pl.when(quarter != p)
            def _():
                landed(mis.at[level, p], ag_r.at[level, p])

    def take_halo(level):
        for side, there in ((0, has_low), (1, has_high)):

            @pl.when(there)
            def _():
                landed(mis_halo.at[level, side], ah_r.at[level, side])

    sub = lax.broadcasted_iota(jnp.int32, (8, BLOCK), 0)
    first, last = sub == 0, sub == 7
    wide = 256

    def to_modes(u, count, weight):
        for c in range(0, columns, wide):
            made = lax.dot_general(
                fs[u, 0:count, c : c + wide], weight[...], (((0,), (0,)), ((), ())), preferred_element_type=F32
            )
            gb[u, PAD + c : PAD + c + wide, :] = made[:, :BLOCK] + made[:, BLOCK:]

    def modes_out(u):
        for c in range(0, columns, 128):
            big, small = split(hb[u, c : c + 128, :])
            gs[u, c : c + 128, 0:BLOCK] = big
            gs[u, c : c + 128, BLOCK:] = small

    def from_modes(u, weight, c):
        return lax.dot_general(
            weight[...], gs[u, c : c + wide, :], (((1,), (1,)), ((), ())), preferred_element_type=F32
        )

    def forward(step, carry):
        level = step // (members // UNROLL)
        for u in range(UNROLL):
            i = step * UNROLL + u
            pltpu.make_async_copy(alpha_hbm.at[0, 0], alpha_v.at[i], in_sem.at[1, i]).wait()
            for c in range(0, columns, 128):
                big, small = split(alpha_v[i, :, c : c + 128])
                fs[u, 0:rows, c : c + 128] = big
                fs[u, rows : 2 * rows, c : c + 128] = small
        for u in range(UNROLL):
            to_modes(u, 2 * rows, w1f)
        for u in range(UNROLL):
            march(gb.at[u], hb.at[u], beta_v[level], first, last, columns)
            modes_out(u)
        for c in range(0, columns, wide):
            total = None
            for u in range(UNROLL):
                i = step * UNROLL + u
                made = from_modes(u, w2f, c)
                made = made[:BLOCK] + made[BLOCK:]
                lh[i, 0, :, c : c + wide] = made[rows : rows + HALO]
                lh[i, 1, :, c : c + wide] = made[rows + HALO :]
                term = made[:rows] * pert_v[i, :, c : c + wide].astype(F32)
                total = term if total is None else total + term
            for q in range(quarters):
                piece = total[q * chunk_rows : (q + 1) * chunk_rows]
                spot = (level, q, slice(None), slice(c, c + wide))
                part[spot] = piece if UNROLL == members else part[spot] + piece

        @pl.when(step == 0)
        def _():
            send_sums(0)
            edges_sent(0)
            send_edges(1)
            send_halo_sums(0)

        return carry

    start_exchange()
    lax.fori_loop(0, fields // UNROLL, forward, 0)
    send_sums(1)
    swap_sums(0)
    send_halo_sums(1)
    send_misfit(0)
    swap_sums(1)
    take_misfit(0)
    send_misfit(1)
    take_halo(0)

    def adjoint(step, carry):
        level = step // (members // UNROLL)

        @pl.when(step == members // UNROLL)
        def _():
            take_misfit(1)
            take_halo(1)

        for u in range(UNROLL):
            i = step * UNROLL + u
            for c in range(0, columns, 128):
                cut = slice(c, c + 128)
                ours = pert_v[i, :, cut].astype(F32)
                pieces = []
                for q in range(quarters):
                    pieces.append(ours[q * chunk_rows : (q + 1) * chunk_rows] * mis[level, q, :, cut])
                for side in range(2):
                    pieces.append(ph[side, i, :, cut] * mis_halo[level, side, :, cut])
                big, small = split(jnp.concatenate(pieces, axis=0))
                fs[u, 0:BLOCK, c : c + 128] = big
                fs[u, BLOCK : 2 * BLOCK, c : c + 128] = small
        for u in range(UNROLL):
            to_modes(u, 2 * BLOCK, w1a)
        for u in range(UNROLL):
            march(gb.at[u], hb.at[u], beta_v[level], first, last, columns)
            modes_out(u)
        for u in range(UNROLL):
            i = step * UNROLL + u
            for c in range(0, columns, wide):
                made = from_modes(u, w2a, c)
                out_v[i, :, c : c + wide] = alpha_v[i, :, c : c + wide] + (made[:rows] + made[rows:])
            pltpu.make_async_copy(out_v.at[i], out_hbm.at[i - level * members, level], out_sem.at[i]).start()
        return carry

    lax.fori_loop(0, fields // UNROLL, adjoint, 0)

    for i in range(fields):
        pltpu.make_async_copy(out_v.at[i], out_hbm.at[i % members, i // members], out_sem.at[i]).wait()
    edges_sent(1)
    for level in range(2):
        pair_copy(level).wait_send()
        for k in range(1, quarters):
            rs_copy(level, k).wait_send()
            ag_copy(level, k).wait_send()

        @pl.when(has_low)
        def _():
            rh_copy(level, 0).wait_send()
            ah_copy(level, 1).wait_send()

        @pl.when(has_high)
        def _():
            rh_copy(level, 1).wait_send()
            ah_copy(level, 0).wait_send()


def local(tiles, groups, alpha, perturbations, innovation, obs_weight, diffusivity):
    members, levels, rows, columns = alpha.shape
    fields = members * levels
    w1f, w2f, w1a, w2a = transforms(rows)
    any_space = pl.BlockSpec(memory_space=pltpu.HBM)
    dma = pltpu.SemaphoreType.DMA
    quarters = groups // 2
    chunk = (rows // quarters, columns)
    halo = (HALO, columns)
    packed = -(-STEPS * members // 8) * 8
    return pl.pallas_call(
        functools.partial(kernel, tiles, groups, members, rows, columns),
        out_shape=jax.ShapeDtypeStruct(alpha.shape, F32),
        in_specs=[pl.BlockSpec(memory_space=pltpu.SMEM)] + [any_space] * 8,
        out_specs=any_space,
        scratch_shapes=[
            pltpu.VMEM((fields, rows, columns), F32),
            pltpu.VMEM((fields, rows, columns), BF16),
            pltpu.VMEM((fields, rows, columns), F32),
            pltpu.VMEM((levels,) + chunk, F32),
            pltpu.VMEM((levels,) + chunk, F32),
            pltpu.VMEM(w1f.shape[1:], BF16),
            pltpu.VMEM(w2f.shape[1:], BF16),
            pltpu.VMEM(w1a.shape[1:], BF16),
            pltpu.VMEM(w2a.shape[1:], BF16),
            pltpu.VMEM((2, levels, packed, columns), F32),
            pltpu.VMEM((2, levels, packed, columns), F32),
            pltpu.VMEM((2, fields, HALO, columns), F32),
            pltpu.VMEM((fields, 2, HALO, columns), F32),
            pltpu.VMEM((levels, quarters) + chunk, F32),
            pltpu.VMEM((levels, 2) + halo, F32),
            pltpu.VMEM((levels, quarters) + chunk, F32),
            pltpu.VMEM((levels, quarters) + halo, F32),
            pltpu.VMEM((levels,) + chunk, F32),
            pltpu.VMEM((levels,) + chunk, F32),
            pltpu.VMEM((levels, quarters) + chunk, F32),
            pltpu.VMEM((levels, 2) + halo, F32),
            pltpu.VMEM((UNROLL, 2 * BLOCK, columns), BF16),
            pltpu.VMEM((UNROLL, PAD + 8 * RUN + PAD, BLOCK), F32),
            pltpu.VMEM((UNROLL, 8 * RUN, BLOCK), F32),
            pltpu.VMEM((UNROLL, 8 * RUN, 2 * BLOCK), BF16),
            pltpu.VMEM((levels, 8, BLOCK), F32),
            pltpu.VMEM((levels, 8, BLOCK), F32),
            dma((2, fields)),
            dma((6,)),
            dma((fields,)),
            dma((levels, 2)),
            dma((levels, 2)),
            dma((levels, quarters)),
            dma((levels, quarters)),
            dma((levels, 2)),
            dma((levels, quarters)),
            dma((levels,)),
            dma((levels,)),
            dma((levels, quarters)),
            dma((levels, quarters)),
            dma((levels, 2)),
            dma((levels, 2)),
        ],
        compiler_params=pltpu.CompilerParams(
            collective_id=0, has_side_effects=True, vmem_limit_bytes=60 * 2**20
        ),
    )(diffusivity, alpha, perturbations, innovation, obs_weight, w1f, w2f, w1a, w2a)


def solution(mesh):
    in_specs = (
        P("mem", None, "grid", None),
        P("mem", None, "grid", None),
        P(None, "grid", None),
        P(None, "grid", None),
        P(),
    )
    out_specs = P("mem", None, "grid", None)
    body = functools.partial(local, mesh.shape["grid"], mesh.shape["mem"])
    return jax.shard_map(body, mesh=mesh, in_specs=in_specs, out_specs=out_specs, check_vma=False)
```

time: 51.8 us -> 45.6 us (0.88)
  the two profiles are of different devices: /device:TPU:98 before, /device:TPU:80 now
where the time goes in v3:
time: 45.6 us; the launch traced here: 45.5 us
  Pallas kernels  41.8 us (92%)
  local copies, waits for them, and re-layouts  3.62 us (8%)
    pallas_call x1, Pallas kernels, local(): pl.pallas_call(functools.partial(kernel, tiles, groups, members, rows, co...  41.8 us
    unnamed x1, local copies, waits for them, and re-layouts  3.62 us

profile of v3, /device:TPU:80, one launch (start us, length us, event | category | flops | bytes accessed | tf_op | source)
XLA Modules:
  0.0 45.5 jit_solution(16929488024513461996)
XLA Ops:
  0.0 41.8 %shard_map.91 = f32[5,2,96,768]{3,2,1,0:T(8,128)} custom-call(f32[2,2]{1,0:T(2,128)} %dif_ref.1, f32[5,2,96,768]{3,2,1,0:T(8,128)} %alpha_hbm.1, bf16[5,2,96,768]{3,2,1,0:T(8,128)(2,1)} %pert_hbm.1, f32[2,96,768]{2,1,0:T(8,128)} %inn_hbm.1, f32[2,96,768]{2,1,0:T(8,128)} %ow_hbm.1, bf16[3,192,256]{2,1,0:T(8,128)(2,1)} %constant.8.clone.w1f_hbm, ...), custom_call_target="tpu_custom_call" | custom-call | tf_op jit(solution)/shard_map/pallas_call | solution.py:436
  41.9 3.6 %copy.11 = f32[5,2,96,768]{3,2,1,0:T(8,128)} copy(f32[5,2,96,768]{3,2,1,0:T(8,128)} %shard_map.91) | data formatting | bytes 5898240

commit v4 on v3

--- a/solution.py
+++ b/solution.py
@@ -40,6 +40,19 @@
             made.append((into, back))
         sets.append((made[0][0], made[1][1], made[1][0], made[0][1]))
     return [np.stack(each) for each in zip(*sets)]
+
+
+def pack(ref, value):
+    third = value.shape[1] // 3
+    ref[0:STEPS] = value[:, : 2 * third]
+    ref[STEPS : STEPS + STEPS // 2, :third] = value[: STEPS // 2, 2 * third :]
+    ref[STEPS : STEPS + STEPS // 2, third:] = value[STEPS // 2 :, 2 * third :]
+
+
+def unpack(block):
+    third = block.shape[1] // 2
+    tail = block[STEPS : STEPS + STEPS // 2]
+    return jnp.concatenate([block[:STEPS], jnp.concatenate([tail[:, :third], tail[:, third:]], axis=0)], axis=1)
 
 
 def split(value):
@@ -78,7 +91,7 @@
     dif_ref, alpha_hbm, pert_hbm, inn_hbm, ow_hbm, w1f_hbm, w2f_hbm, w1a_hbm, w2a_hbm,
     out_hbm,
     alpha_v, pert_v, out_v, inn_v, ow_v, w1f, w2f, w1a, w2a,
-    edge, edge_got, ph, lh, part, halo_part, got, halo_got, mine, other, mis, mis_halo,
+    edge, edge_got, ph, lh, part, halo_part, got, halo_got, mine, other, mis, mis_halo, mis_edge, mis_got,
     fs, gb, hb, gs, beta_v, scale_v,
     in_sem, w_sem, out_sem, ph_s, ph_r, rs_s, rs_r, rh_s, rh_r, x_s, x_r, ag_s, ag_r, ah_s, ah_r,
 ):
@@ -133,13 +146,9 @@
     gb[...] = jnp.zeros_like(gb)
     ph[...] = jnp.zeros_like(ph)
 
-    @pl.when(g == 0)
-    def _():
-        mis_halo[:, 0] = jnp.zeros_like(mis_halo[:, 0])
-
-    @pl.when(g == tiles - 1)
-    def _():
-        mis_halo[:, 1] = jnp.zeros_like(mis_halo[:, 1])
+    mis_halo[...] = jnp.zeros_like(mis_halo)
+    halo_part[...] = jnp.zeros_like(halo_part)
+    mis_edge[...] = jnp.zeros_like(mis_edge)
 
     for i in range(fields):
         loads[i].wait()
@@ -176,6 +185,7 @@
         neighbours = jnp.minimum(g, 1) + jnp.minimum(tiles - 1 - g, 1)
         pl.semaphore_wait(barrier, quarters + neighbours)
         send_edges(0)
+        send_edges(1)
 
     for copy in weights:
         copy.wait()
@@ -210,12 +220,11 @@
             device_id=(g, 2 * peer + half), device_id_type=MESH,
         )
 
-    def ah_copy(level, side):
-        first = (chunk_rows - HALO) * (1 - side)
+    def ah_copy(level, side, p):
         return pltpu.make_async_remote_copy(
-            src_ref=mis.at[level, (quarters - 1) * (1 - side), pl.ds(first, HALO)], dst_ref=mis_halo.at[level, side],
-            send_sem=ah_s.at[level, side], recv_sem=ah_r.at[level, side],
-            device_id=(g + 1 - 2 * side, m), device_id_type=MESH,
+            src_ref=mis_edge.at[level, side], dst_ref=mis_got.at[level, side],
+            send_sem=ah_s.at[level, side, p], recv_sem=ah_r.at[level, side],
+            device_id=(g + 1 - 2 * side, 2 * p + half), device_id_type=MESH,
         )
 
     def landed(ref, sem):
@@ -240,7 +249,8 @@
                     i = level * members + f
                     term = lh[i, side] * ph[side, i]
                     total = term if total is None else total + term
-                halo_part[level, side] = total
+                inner = (HALO - STEPS) * (1 - side)
+                pack(halo_part.at[level, side], total[inner : inner + STEPS])
                 rh_copy(level, side).start()
 
     at_low = (quarter == 0) & has_low
@@ -254,14 +264,14 @@
         for p in peers:
             total = total + got[level, p]
         mine[level] = total
-        for there, first in ((at_low, 0), (at_high, chunk_rows - HALO)):
+        for there, begin in ((at_low, 0), (at_high, chunk_rows - STEPS)):
 
             @pl.when(there)
             def _():
                 for p in range(quarters):
                     landed(halo_got.at[level, p], rh_r.at[level, p])
-                spot = slice(first, first + HALO)
-                mine[level, spot] = mine[level, spot] + sum(halo_got[level, p] for p in range(quarters))
+                spot = slice(begin, begin + STEPS)
+                mine[level, spot] = mine[level, spot] + unpack(sum(halo_got[level, p] for p in range(quarters)))
 
         pair_copy(level).start()
 
@@ -271,30 +281,27 @@
         mis[level, quarter] = ow_v[level] * ((mine[level] + other[level]) * scale - inn_v[level]) * scale
         for k in range(1, quarters):
             ag_copy(level, k).start()
+        for there, side, begin in ((at_low, 1, 0), (at_high, 0, chunk_rows - STEPS)):
+
+            @pl.when(there)
+            def _():
+                pack(mis_edge.at[level, side], mis[level, quarter, begin : begin + STEPS])
+                for p in range(quarters):
+                    ah_copy(level, side, p).start()
 
     def take_misfit(level):
-        for p in (0, quarters - 1):
-
-            @pl.when(quarter != p)
-            def _():
-                landed(mis.at[level, p], ag_r.at[level, p])
-
-            @pl.when(has_low if p == 0 else has_high)
-            def _():
-                ah_copy(level, 1 if p == 0 else 0).start()
-
-        for p in range(1, quarters - 1):
-
-            @pl.when(quarter != p)
-            def _():
-                landed(mis.at[level, p], ag_r.at[level, p])
+        for k in range(1, quarters):
+            p = lax.rem(quarter + k, quarters)
+            landed(mis.at[level, p], ag_r.at[level, p])
 
     def take_halo(level):
         for side, there in ((0, has_low), (1, has_high)):
 
             @pl.when(there)
             def _():
-                landed(mis_halo.at[level, side], ah_r.at[level, side])
+                landed(mis_got.at[level, side], ah_r.at[level, side])
+                inner = (HALO - STEPS) * (1 - side)
+                mis_halo[level, side, inner : inner + STEPS] = unpack(mis_got[level, side])
 
     sub = lax.broadcasted_iota(jnp.int32, (8, BLOCK), 0)
     first, last = sub == 0, sub == 7
@@ -318,24 +325,22 @@
             weight[...], gs[u, c : c + wide, :], (((1,), (1,)), ((), ())), preferred_element_type=F32
         )
 
-    def forward(step, carry):
-        level = step // (members // UNROLL)
-        for u in range(UNROLL):
-            i = step * UNROLL + u
-            pltpu.make_async_copy(alpha_hbm.at[0, 0], alpha_v.at[i], in_sem.at[1, i]).wait()
+    def forward(level, begin, count):
+        batch = [(u, level * members + begin + u) for u in range(count)]
+        for u, i in batch:
+            loads[fields + i].wait()
             for c in range(0, columns, 128):
                 big, small = split(alpha_v[i, :, c : c + 128])
                 fs[u, 0:rows, c : c + 128] = big
                 fs[u, rows : 2 * rows, c : c + 128] = small
-        for u in range(UNROLL):
+        for u, i in batch:
             to_modes(u, 2 * rows, w1f)
-        for u in range(UNROLL):
+        for u, i in batch:
             march(gb.at[u], hb.at[u], beta_v[level], first, last, columns)
             modes_out(u)
         for c in range(0, columns, wide):
             total = None
-            for u in range(UNROLL):
-                i = step * UNROLL + u
+            for u, i in batch:
                 made = from_modes(u, w2f, c)
                 made = made[:BLOCK] + made[BLOCK:]
                 lh[i, 0, :, c : c + wide] = made[rows : rows + HALO]
@@ -345,38 +350,16 @@
             for q in range(quarters):
                 piece = total[q * chunk_rows : (q + 1) * chunk_rows]
                 spot = (level, q, slice(None), slice(c, c + wide))
-                part[spot] = piece if UNROLL == members else part[spot] + piece
-
-        @pl.when(step == 0)
-        def _():
-            send_sums(0)
-            edges_sent(0)
-            send_edges(1)
-            send_halo_sums(0)
-
-        return carry
-
-    start_exchange()
-    lax.fori_loop(0, fields // UNROLL, forward, 0)
-    send_sums(1)
-    swap_sums(0)
-    send_halo_sums(1)
-    send_misfit(0)
-    swap_sums(1)
-    take_misfit(0)
-    send_misfit(1)
-    take_halo(0)
-
-    def adjoint(step, carry):
-        level = step // (members // UNROLL)
-
-        @pl.when(step == members // UNROLL)
+                part[spot] = piece if begin == 0 else part[spot] + piece
+
+    def adjoint(level, carry):
+        @pl.when(level == 1)
         def _():
             take_misfit(1)
             take_halo(1)
 
-        for u in range(UNROLL):
-            i = step * UNROLL + u
+        batch = [(u, level * members + u) for u in range(members)]
+        for u, i in batch:
             for c in range(0, columns, 128):
                 cut = slice(c, c + 128)
                 ours = pert_v[i, :, cut].astype(F32)
@@ -388,25 +371,38 @@
                 big, small = split(jnp.concatenate(pieces, axis=0))
                 fs[u, 0:BLOCK, c : c + 128] = big
                 fs[u, BLOCK : 2 * BLOCK, c : c + 128] = small
-        for u in range(UNROLL):
+        for u, i in batch:
             to_modes(u, 2 * BLOCK, w1a)
-        for u in range(UNROLL):
+        for u, i in batch:
             march(gb.at[u], hb.at[u], beta_v[level], first, last, columns)
             modes_out(u)
-        for u in range(UNROLL):
-            i = step * UNROLL + u
+        for u, i in batch:
             for c in range(0, columns, wide):
                 made = from_modes(u, w2a, c)
                 out_v[i, :, c : c + wide] = alpha_v[i, :, c : c + wide] + (made[:rows] + made[rows:])
-            pltpu.make_async_copy(out_v.at[i], out_hbm.at[i - level * members, level], out_sem.at[i]).start()
+            pltpu.make_async_copy(out_v.at[i], out_hbm.at[u, level], out_sem.at[i]).start()
         return carry
 
-    lax.fori_loop(0, fields // UNROLL, adjoint, 0)
+    start_exchange()
+    forward(0, 0, members)
+    send_sums(0)
+    forward(1, 0, 2)
+    send_halo_sums(0)
+    forward(1, 2, members - 2)
+    send_sums(1)
+    send_halo_sums(1)
+    swap_sums(0)
+    send_misfit(0)
+    swap_sums(1)
+    send_misfit(1)
+    take_misfit(0)
+    take_halo(0)
+    lax.fori_loop(0, 2, adjoint, 0)
 
     for i in range(fields):
         pltpu.make_async_copy(out_v.at[i], out_hbm.at[i % members, i // members], out_sem.at[i]).wait()
-    edges_sent(1)
     for level in range(2):
+        edges_sent(level)
         pair_copy(level).wait_send()
         for k in range(1, quarters):
             rs_copy(level, k).wait_send()
@@ -415,12 +411,17 @@
         @pl.when(has_low)
         def _():
             rh_copy(level, 0).wait_send()
-            ah_copy(level, 1).wait_send()
 
         @pl.when(has_high)
         def _():
             rh_copy(level, 1).wait_send()
-            ah_copy(level, 0).wait_send()
+
+        for there, side in ((at_low, 1), (at_high, 0)):
+
+            @pl.when(there)
+            def _():
+                for p in range(quarters):
+                    ah_copy(level, side, p).wait_send()
 
 
 def local(tiles, groups, alpha, perturbations, innovation, obs_weight, diffusivity):
@@ -432,8 +433,9 @@
     quarters = groups // 2
     chunk = (rows // quarters, columns)
     halo = (HALO, columns)
+    dense = (HALO, columns // 3 * 2)
     packed = -(-STEPS * members // 8) * 8
-    return pl.pallas_call(
+    made = pl.pallas_call(
         functools.partial(kernel, tiles, groups, members, rows, columns),
         out_shape=jax.ShapeDtypeStruct(alpha.shape, F32),
         in_specs=[pl.BlockSpec(memory_space=pltpu.SMEM)] + [any_space] * 8,
@@ -453,13 +455,15 @@
             pltpu.VMEM((2, fields, HALO, columns), F32),
             pltpu.VMEM((fields, 2, HALO, columns), F32),
             pltpu.VMEM((levels, quarters) + chunk, F32),
-            pltpu.VMEM((levels, 2) + halo, F32),
+            pltpu.VMEM((levels, 2) + dense, F32),
             pltpu.VMEM((levels, quarters) + chunk, F32),
-            pltpu.VMEM((levels, quarters) + halo, F32),
+            pltpu.VMEM((levels, quarters) + dense, F32),
             pltpu.VMEM((levels,) + chunk, F32),
             pltpu.VMEM((levels,) + chunk, F32),
             pltpu.VMEM((levels, quarters) + chunk, F32),
             pltpu.VMEM((levels, 2) + halo, F32),
+            pltpu.VMEM((levels, 2) + dense, F32),
+            pltpu.VMEM((levels, 2) + dense, F32),
             pltpu.VMEM((UNROLL, 2 * BLOCK, columns), BF16),
             pltpu.VMEM((UNROLL, PAD + 8 * RUN + PAD, BLOCK), F32),
             pltpu.VMEM((UNROLL, 8 * RUN, BLOCK), F32),
@@ -479,13 +483,34 @@
             dma((levels,)),
             dma((levels, quarters)),
             dma((levels, quarters)),
-            dma((levels, 2)),
+            dma((levels, 2, quarters)),
             dma((levels, 2)),
         ],
         compiler_params=pltpu.CompilerParams(
             collective_id=0, has_side_effects=True, vmem_limit_bytes=60 * 2**20
         ),
     )(diffusivity, alpha, perturbations, innovation, obs_weight, w1f, w2f, w1a, w2a)
+    return pl.pallas_call(
+        pass_on,
+        out_shape=jax.ShapeDtypeStruct(alpha.shape, F32),
+        in_specs=[any_space],
+        out_specs=any_space,
+        scratch_shapes=[pltpu.VMEM(alpha.shape, F32), dma((2, fields))],
+        compiler_params=pltpu.CompilerParams(vmem_limit_bytes=60 * 2**20),
+    )(made)
+
+
+def pass_on(src, dst, held, sem):
+    fields = [(i, j) for i in range(src.shape[0]) for j in range(src.shape[1])]
+    reads = [pltpu.make_async_copy(src.at[f], held.at[f], sem.at[0, n]) for n, f in enumerate(fields)]
+    writes = [pltpu.make_async_copy(held.at[f], dst.at[f], sem.at[1, n]) for n, f in enumerate(fields)]
+    for copy in reads:
+        copy.start()
+    for read, write in zip(reads, writes):
+        read.wait()
+        write.start()
+    for copy in writes:
+        copy.wait()
 
 
 def solution(mesh):

time: 45.6 us -> 40.8 us (0.89)
  local copies, waits for them, and re-layouts: 3.62 us -> 0 us
  Pallas kernels: 41.8 us -> 40.4 us
    pallas_call x1, Pallas kernels: 41.8 us -> 37.6 us  [local(): pl.pallas_call(functools.partial(kernel, tiles, groups, members, rows, co...]
    unnamed x1 -> x0, local copies, waits for them, and re-layouts: 3.62 us -> none
    pallas_call x0 -> x1, Pallas kernels: none -> 2.72 us  [local(): pl.pallas_call(pass_on, out_shape=jax.ShapeDtypeStruct(alpha.shape, F32),...]
where the time goes in v4:
time: 40.8 us; the launch traced here: 40.5 us
  Pallas kernels  40.4 us (99%)
    pallas_call x1, Pallas kernels, local(): pl.pallas_call(functools.partial(kernel, tiles, groups, members, rows, co...  37.6 us
    pallas_call x1, Pallas kernels, local(): pl.pallas_call(pass_on, out_shape=jax.ShapeDtypeStruct(alpha.shape, F32),...  2.72 us

profile of v4, /device:TPU:80, one launch (start us, length us, event | category | flops | bytes accessed | tf_op | source)
XLA Modules:
  0.0 40.5 jit_solution(705339632725215980)
XLA Ops:
  0.0 37.6 %shard_map.91.src = f32[5,2,96,768]{3,2,1,0:T(8,128)} custom-call(f32[2,2]{1,0:T(2,128)} %dif_ref.1, f32[5,2,96,768]{3,2,1,0:T(8,128)} %alpha_hbm.1, bf16[5,2,96,768]{3,2,1,0:T(8,128)(2,1)} %pert_hbm.1, f32[2,96,768]{2,1,0:T(8,128)} %inn_hbm.1, f32[2,96,768]{2,1,0:T(8,128)} %ow_hbm.1, bf16[3,192,256]{2,1,0:T(8,128)(2,1)} %constant.8.clone.w1f_hbm, ...), custom_call_target="tpu_custom_call" | custom-call | tf_op jit(solution)/shard_map/pallas_call | solution.py:438
  37.6 2.7 %shard_map.92 = f32[5,2,96,768]{3,2,1,0:T(8,128)} custom-call(f32[5,2,96,768]{3,2,1,0:T(8,128)} %shard_map.91.src), custom_call_target="tpu_custom_call" | custom-call | tf_op jit(solution)/shard_map/pallas_call | solution.py:493

commit v5 on v4

--- a/solution.py
+++ b/solution.py
@@ -185,7 +185,6 @@
         neighbours = jnp.minimum(g, 1) + jnp.minimum(tiles - 1 - g, 1)
         pl.semaphore_wait(barrier, quarters + neighbours)
         send_edges(0)
-        send_edges(1)
 
     for copy in weights:
         copy.wait()
@@ -279,8 +278,6 @@
         landed(other.at[level], x_r.at[level])
         scale = scale_v[level, 0:1, 0:1]
         mis[level, quarter] = ow_v[level] * ((mine[level] + other[level]) * scale - inn_v[level]) * scale
-        for k in range(1, quarters):
-            ag_copy(level, k).start()
         for there, side, begin in ((at_low, 1, 0), (at_high, 0, chunk_rows - STEPS)):
 
             @pl.when(there)
@@ -288,6 +285,9 @@
                 pack(mis_edge.at[level, side], mis[level, quarter, begin : begin + STEPS])
                 for p in range(quarters):
                     ah_copy(level, side, p).start()
+
+        for k in range(1, quarters):
+            ag_copy(level, k).start()
 
     def take_misfit(level):
         for k in range(1, quarters):
@@ -385,6 +385,8 @@
 
     start_exchange()
     forward(0, 0, members)
+    edges_sent(0)
+    send_edges(1)
     send_sums(0)
     forward(1, 0, 2)
     send_halo_sums(0)
@@ -401,8 +403,8 @@
 
     for i in range(fields):
         pltpu.make_async_copy(out_v.at[i], out_hbm.at[i % members, i // members], out_sem.at[i]).wait()
+    edges_sent(1)
     for level in range(2):
-        edges_sent(level)
         pair_copy(level).wait_send()
         for k in range(1, quarters):
             rs_copy(level, k).wait_send()

time: 40.8 us -> 40.3 us (0.988)
  no operation moved by 1% of the time
where the time goes in v5:
time: 40.3 us; the launch traced here: 40.2 us
  Pallas kernels  40 us (99%)
    pallas_call x1, Pallas kernels, local(): pl.pallas_call(functools.partial(kernel, tiles, groups, members, rows, co...  37.3 us
    pallas_call x1, Pallas kernels, local(): pl.pallas_call(pass_on, out_shape=jax.ShapeDtypeStruct(alpha.shape, F32),...  2.72 us

profile of v5, /device:TPU:80, one launch (start us, length us, event | category | flops | bytes accessed | tf_op | source)
XLA Modules:
  0.0 40.2 jit_solution(12057581353746596948)
XLA Ops:
  0.0 37.3 %shard_map.91.src = f32[5,2,96,768]{3,2,1,0:T(8,128)} custom-call(f32[2,2]{1,0:T(2,128)} %dif_ref.1, f32[5,2,96,768]{3,2,1,0:T(8,128)} %alpha_hbm.1, bf16[5,2,96,768]{3,2,1,0:T(8,128)(2,1)} %pert_hbm.1, f32[2,96,768]{2,1,0:T(8,128)} %inn_hbm.1, f32[2,96,768]{2,1,0:T(8,128)} %ow_hbm.1, bf16[3,192,256]{2,1,0:T(8,128)(2,1)} %constant.8.clone.w1f_hbm, ...), custom_call_target="tpu_custom_call" | custom-call | tf_op jit(solution)/shard_map/pallas_call | solution.py:440
  37.3 2.7 %shard_map.92 = f32[5,2,96,768]{3,2,1,0:T(8,128)} custom-call(f32[5,2,96,768]{3,2,1,0:T(8,128)} %shard_map.91.src), custom_call_target="tpu_custom_call" | custom-call | tf_op jit(solution)/shard_map/pallas_call | solution.py:495
